TPU v7x, 128 devices: a whole 4x4x4 slice. The times are simulated.
128 devices in a mesh: seq: 4 (over z_lo, core), fsdp: 32 (over y, z_hi, x).
Axes of the slice: x: 4, y: 4, z: 4 (z_hi: 2, z_lo: 2; z = z_hi * 2 + z_lo), core: 2. Of those that a mesh axis runs over, the one named last changes fastest.
Arguments:
- tokens: bfloat16 [32, 1024, 1024], P('fsdp', 'seq'), may hold values from -6 to 6
- triple: bfloat16 [1024, 3072], P('fsdp'), may hold values from -0.25 to 0.25
- triple_bias: bfloat16 [3072], P('fsdp'), may hold values from -1.796875 to 1.796875
- merger: bfloat16 [1024, 1024], P('fsdp'), may hold values from -0.75 to 0.75
- merger_bias: bfloat16 [1024], P('fsdp'), may hold values from -1.796875 to 1.796875
- first_gain: bfloat16 [1024], P('fsdp'), may hold values from 0.25 to 1.75
- first_shift: bfloat16 [1024], P('fsdp'), may hold values from -1.796875 to 1.796875
- expand: bfloat16 [1024, 4096], P('fsdp'), may hold values from -0.1875 to 0.1875
- expand_bias: bfloat16 [4096], P('fsdp'), may hold values from -1.796875 to 1.796875
- shrink: bfloat16 [4096, 1024], P('fsdp'), may hold values from -0.09375 to 0.09375
- shrink_bias: bfloat16 [1024], P('fsdp'), may hold values from -1.796875 to 1.796875
- second_gain: bfloat16 [1024], P('fsdp'), may hold values from 0.25 to 1.75
- second_shift: bfloat16 [1024], P('fsdp'), may hold values from -1.796875 to 1.796875
- cotangent: bfloat16 [32, 1024, 1024], P('fsdp', 'seq'), may hold values from -6 to 6
Outputs:
- encoded: bfloat16 [32, 1024, 1024], P('fsdp', 'seq')
- tokens_grad: bfloat16 [32, 1024, 1024], P('fsdp', 'seq')
- triple_grad: float32 [1024, 3072], P('fsdp')
- triple_bias_grad: float32 [3072], P('fsdp')
- merger_grad: float32 [1024, 1024], P('fsdp')
- merger_bias_grad: float32 [1024], P('fsdp')
- first_gain_grad: float32 [1024], P('fsdp')
- first_shift_grad: float32 [1024], P('fsdp')
- expand_grad: float32 [1024, 4096], P('fsdp')
- expand_bias_grad: float32 [4096], P('fsdp')
- shrink_grad: float32 [4096, 1024], P('fsdp')
- shrink_bias_grad: float32 [1024], P('fsdp')
- second_gain_grad: float32 [1024], P('fsdp')
- second_shift_grad: float32 [1024], P('fsdp')
All inputs are finite; a program needn't handle non-finite values.
Results may differ from a plain program's by a relative error of at most 0.025.
Values may be sent and summed in bfloat16 or wider, within the bound.
A program may use at most 192 MiB of HBM per device.

v0:
```python
import functools
import math

import jax
import jax.numpy as jnp
import numpy as np
from jax import lax
from jax.experimental import pallas as pl
from jax.experimental.pallas import tpu as pltpu
from jax.sharding import PartitionSpec as P

HEADS = 16
D = 1024
FF = 4096
LENGTH = 1024
HEAD = 64
bf16 = jnp.bfloat16
f32 = jnp.float32
norm_epsilon = 1e-05
MESH = pl.DeviceIdType.MESH
ANY = pl.BlockSpec(memory_space=pl.ANY)
VMEM = pl.BlockSpec(memory_space=pltpu.VMEM)
SIBLING = [(0, 1), (1, 0), (2, 3), (3, 2)]
ACROSS = [(0, 2), (2, 0), (1, 3), (3, 1)]


class Place:
    def __init__(self):
        seq, fsdp = lax.axis_index("seq"), lax.axis_index("fsdp")
        self.seq, self.fsdp = seq, fsdp
        self.z_lo, self.core = lax.div(seq, 2), lax.rem(seq, 2)
        self.x, rest = lax.rem(fsdp, 4), lax.div(fsdp, 4)
        self.z_hi, self.y = lax.rem(rest, 2), lax.div(rest, 2)

    def at(self, y=None, z_hi=None, x=None, z_lo=None, core=None):
        y = self.y if y is None else y
        z_hi = self.z_hi if z_hi is None else z_hi
        x = self.x if x is None else x
        z_lo = self.z_lo if z_lo is None else z_lo
        core = self.core if core is None else core
        return {"seq": z_lo * 2 + core, "fsdp": (y * 2 + z_hi) * 4 + x}

    def along_x(self, k):
        return lax.rem(self.x + k, 4)

    def along_y(self, k):
        return lax.rem(self.y + k, 4)

    def z_others(self):
        return [
            self.at(z_lo=1 - self.z_lo),
            self.at(z_hi=1 - self.z_hi, z_lo=1 - self.z_lo),
            self.at(z_hi=1 - self.z_hi),
        ]


def meet(peers):
    barrier = pltpu.get_barrier_semaphore()
    for peer in peers:
        pl.semaphore_signal(barrier, inc=1, device_id=peer, device_id_type=MESH)
    pl.semaphore_wait(barrier, len(peers))


class Wires:
    def __init__(self, send, recv):
        self.send, self.recv, self.used, self.open = send, recv, 0, []

    def make(self, source, target, device):
        assert self.used < self.send.shape[0]
        copy = pltpu.make_async_remote_copy(
            src_ref=source,
            dst_ref=target,
            send_sem=self.send.at[self.used],
            recv_sem=self.recv.at[self.used],
            device_id=device,
            device_id_type=MESH,
        )
        self.used += 1
        return copy

    def go(self, source, target, device):
        copy = self.make(source, target, device)
        copy.start()
        self.open.append(copy)
        return copy

    def drain(self):
        for copy in self.open:
            copy.wait_send()
        self.open = []


def arrive(copies):
    for copy in copies:
        copy.wait_recv()


def gather_steps(wires, me, whole):
    half = whole.shape[-1] // 2
    rows = whole.shape[-2] // 2
    low, high, both = pl.ds(0, rows), pl.ds(rows, rows), pl.ds(0, 2 * rows)
    left, right = pl.ds(0, half), pl.ds(half, half)
    on_x = (me.x, lambda i: me.at(x=i))
    on_y = (me.y, lambda i: me.at(y=i))
    hops = (
        (
            (*on_x, lambda i, r: whole.at[me.y, :, i, r, left]),
            (*on_y, lambda i, r: whole.at[i, :, me.x, r, right]),
        ),
        (
            (*on_y, lambda i, r: whole.at[i, :, :, r, left]),
            (*on_x, lambda i, r: whole.at[:, :, i, r, right]),
        ),
    )
    for hop in hops:
        direct = []
        for here, device, piece in hop:
            up, down = lax.rem(here + 1, 4), lax.rem(here + 3, 4)
            direct.append(
                (
                    wires.go(piece(here, both), piece(here, both), device(up)),
                    wires.go(piece(here, both), piece(here, both), device(down)),
                )
            )
        yield
        relayed = []
        for (here, device, piece), (from_down, from_up) in zip(hop, direct):
            up, down = lax.rem(here + 1, 4), lax.rem(here + 3, 4)
            from_down.wait_recv()
            relayed.append(wires.go(piece(down, low), piece(down, low), device(up)))
            from_up.wait_recv()
            relayed.append(wires.go(piece(up, high), piece(up, high), device(down)))
        yield
        arrive(relayed)
    yield


def dot(a, b, dims):
    return lax.dot_general(a, b, (dims, ((), ())), preferred_element_type=f32)


def turn(block, cosine, sine):
    lane = lax.broadcasted_iota(jnp.int32, block.shape, 1)
    other = jnp.where(
        lax.rem(lane, 64) < 32, pltpu.roll(block, 96, 1), pltpu.roll(block, 32, 1)
    )
    return block * cosine + other * sine


def row_norm(rows):
    centered = rows - jnp.mean(rows, axis=-1, keepdims=True)
    scale = lax.rsqrt(jnp.mean(centered * centered, axis=-1, keepdims=True) + norm_epsilon)
    return centered * scale, scale


def row_norm_backward(upstream, gain, n, scale):
    u = upstream * gain
    mean = jnp.mean(u, axis=-1, keepdims=True)
    along = jnp.mean(u * n, axis=-1, keepdims=True)
    return scale * (u - mean - n * along)


class Saves:
    def __init__(self, sems):
        self.sems, self.used, self.open = sems, 0, []

    def go(self, source, target):
        assert self.used < self.sems.shape[0]
        copy = pltpu.make_async_copy(source, target, self.sems.at[self.used])
        self.used += 1
        copy.start()
        self.open.append(copy)
        return copy

    def wait(self, copy):
        copy.wait()
        self.open = [other for other in self.open if other is not copy]

    def drain(self):
        for copy in self.open:
            copy.wait()
        self.open = []


def forward_kernel(
    triple, expand, shrink, merger, small, tokens, cotangent, cosines, sines,
    whole_t, whole_e, whole_s, whole_m, sequence, small_full, encoded, small_grads,
    e_out, o_out, q_out, k_out, v_out, r_out, ctx_out, n_out, scale_out, low_out,
    active_out, slope_out, second_out, feed_out,
    small_x, small_y, small_z, sum_x, sum_y, wt, we, ws, wm, seq, ups,
    e_buf, o_buf, q_buf, k_buf, v_buf, r_buf, ctx, part, give_a, take_a, give_f, take_f,
    n_buf, scale_buf, low_buf, active_buf, slope_buf, second_buf, feed_buf,
    send, recv, local_sems,
):
    me = Place()
    wires, saves = Wires(send, recv), Saves(local_sems)
    sibling = me.at(core=1 - me.core)
    across = me.at(z_lo=1 - me.z_lo)
    partner = me.at(z_hi=1 - me.z_hi, z_lo=1 - me.z_lo)
    peers = [sibling, across, partner]
    peers += [me.at(x=me.along_x(k)) for k in (1, 2, 3)]
    peers += [me.at(y=me.along_y(k)) for k in (1, 2, 3)]
    meet(peers)

    mine_here = me.core == me.z_hi
    slot_t = whole_t.at[me.y, me.z_hi, me.x]
    slot_e = whole_e.at[me.y, me.z_hi, me.x]
    slot_s = whole_s.at[me.y, 0, me.x]
    slot_m = whole_m.at[me.y, 0, me.x]
    z_t = wires.go(triple.at[1 - me.z_lo, me.core], slot_t, partner)
    tok_across = wires.go(tokens, seq.at[me.seq], across)
    x_small = [wires.go(small, small_x.at[k - 1], me.at(x=me.along_x(k))) for k in (1, 2, 3)]
    tok_beside = wires.go(tokens, seq.at[me.seq], sibling)
    z_e = wires.go(expand.at[me.core], slot_e, partner)
    cot_beside = wires.go(cotangent, ups.at[me.core], sibling)
    own_t = saves.go(triple.at[me.z_lo, me.core], slot_t)
    own_tok = saves.go(tokens, seq.at[me.seq])
    own_e = saves.go(expand.at[me.core], slot_e)
    own_cot = saves.go(cotangent, ups.at[me.core])
    z_s = wires.make(shrink, slot_s, partner)
    z_m = wires.make(merger, slot_m, partner)
    own_s = pltpu.make_async_copy(shrink, slot_s, local_sems.at[40])
    own_m = pltpu.make_async_copy(merger, slot_m, local_sems.at[41])

    @pl.when(mine_here)
    def _():
        z_s.start()
        z_m.start()
        own_s.start()
        own_m.start()

    go_t = gather_steps(wires, me, whole_t)
    go_e = gather_steps(wires, me, whole_e)
    go_s = gather_steps(wires, me, whole_s)
    go_m = gather_steps(wires, me, whole_m)
    saves.wait(own_t)
    z_t.wait_recv()
    next(go_t)
    arrive(x_small)
    sum_x[...] = small[...] + small_x[0] + small_x[1] + small_x[2]
    y_small = [wires.go(sum_x, small_y.at[k - 1], me.at(y=me.along_y(k))) for k in (1, 2, 3)]
    next(go_t)
    arrive(y_small)
    sum_y[...] = sum_x[...] + small_y[0] + small_y[1] + small_y[2]
    z_small = wires.go(sum_y, small_z, partner)
    next(go_t)
    saves.wait(own_e)
    z_e.wait_recv()
    next(go_e)

    @pl.when(mine_here)
    def _():
        own_s.wait()
        own_m.wait()

    @pl.when(jnp.logical_not(mine_here))
    def _():
        z_s.wait_recv()
        z_m.wait_recv()

    next(go_m)
    tok_across.wait_recv()
    far = seq.at[(1 - me.z_lo) * 2 + me.core]
    tok_relay = wires.go(far, far, sibling)
    z_small.wait_recv()
    small_full[...] = sum_y[...] + small_z[...]
    next(go_t)
    next(go_e)
    next(go_m)
    next(go_s)
    next(go_t)
    load_t = saves.go(whole_t, wt)
    next(go_e)
    next(go_m)
    next(go_s)
    saves.wait(own_tok)
    arrive([tok_beside, tok_relay])
    saves.wait(load_t)

    def bias(row, start, n):
        return small_full[pl.ds(row, 1), pl.ds(pl.multiple_of(start, 128), n)]

    bias_t = [
        bias(t, me.z_lo * 512 + j * 256 + me.core * 128, 128) for t in range(3) for j in range(2)
    ]
    bias_t = jnp.concatenate(bias_t, axis=1)

    def project(i, carry):
        rows = pl.ds(pl.multiple_of(i * 256, 256), 256)
        pre = dot(seq[i], wt[...].reshape(D, 768), NN) + bias_t
        cosine, sine = cosines[rows, :], sines[rows, :]
        for p in range(2):
            cut = pre[:, p * 128 : p * 128 + 128]
            q_buf[p, rows, :] = (turn(cut, cosine, sine) * 0.125).astype(bf16)
            cut = pre[:, 256 + p * 128 : 384 + p * 128]
            k_buf[p, rows, :] = turn(cut, cosine, sine).astype(bf16)
            v_buf[p, rows, pl.ds(0, 128)] = pre[:, 512 + p * 128 : 640 + p * 128].astype(bf16)
            v_buf[p, rows, pl.ds(128, 128)] = jnp.ones((256, 128), bf16)
        return carry

    lax.fori_loop(0, 4, project, 0)
    saves.go(seq, sequence)
    saves.go(q_buf, q_out)
    saves.go(k_buf, k_out)
    saves.go(v_buf, v_out)
    next(go_s)
    ctx_copies = []
    for p in range(2):

        def attend(i, carry, p=p):
            rows = pl.ds(pl.multiple_of(i * 256, 256), 256)
            lane = lax.broadcasted_iota(jnp.int32, (256, 128), 1)
            found = []
            for h in range(2):
                head = (lane >= 64) if h else (lane < 64)
                q = jnp.where(head, q_buf[p, rows, :], jnp.zeros((), bf16))
                scores = dot(q, k_buf[p], NT)
                peak = jnp.max(scores, axis=1, keepdims=True)
                powers = jnp.exp(scores - peak).astype(bf16)
                e_buf[2 * p + h, rows, :] = powers
                found.append(dot(powers, v_buf[p], NN))
            first = lane < 64
            over = 1.0 / jnp.where(first, found[0][:, 128:], found[1][:, 128:])
            r_buf[p, rows, :] = over
            o_buf[p, rows, :] = (jnp.where(first, found[0][:, :128], found[1][:, :128]) * over).astype(bf16)
            return carry

        lax.fori_loop(0, 4, attend, 0)
        saves.go(e_buf.at[pl.ds(2 * p, 2)], e_out.at[pl.ds(2 * p, 2)])
        theirs = o_buf.at[p, pl.ds(pl.multiple_of((1 - me.z_lo) * 512, 512), 512)]
        ours = o_buf.at[p, pl.ds(pl.multiple_of(me.z_lo * 512, 512), 512)]
        ctx_copies.append(wires.go(theirs, ctx.at[me.z_lo, p], across))
        keep = saves.go(ours, ctx.at[me.z_lo, p])
        if p == 0:
            next(go_e)
            next(go_m)
            keep_0 = keep
    saves.go(r_buf, r_out)
    saves.go(o_buf, o_out)
    next(go_m)
    load_m = saves.go(whole_m, wm)
    next(go_s)
    saves.wait(keep_0)
    saves.wait(keep)
    arrive(ctx_copies)
    saves.wait(load_m)
    ctx_rows = jnp.concatenate([ctx[0, 0], ctx[0, 1], ctx[1, 0], ctx[1, 1]], axis=1)
    merge = []
    for i in range(2):
        rows = pl.ds(i * 256, 256)
        found = dot(ctx_rows[i * 256 : i * 256 + 256], wm[...].reshape(512, D), NN)
        part[rows, :] = found
        give_a[rows, :] = found.astype(bf16)
        merge.append(wires.go(give_a.at[rows], take_a.at[rows], sibling))
    saves.go(ctx, ctx_out)
    next(go_e)
    load_e = saves.go(whole_e, we)
    bias_m, gain_1, shift_1 = bias(3, 0, D), bias(4, 0, D), bias(5, 0, D)

    def first_norm(i, carry):
        rows = pl.ds(pl.multiple_of(i * 64, 64), 64)
        at = pl.ds(pl.multiple_of(lax.rem(i, 4) * 64, 64), 64)
        inputs = seq[me.z_lo * 2 + lax.div(i, 4), at, :].astype(f32)
        total = inputs + part[rows, :] + take_a[rows, :].astype(f32) + bias_m
        n, scale = row_norm(total)
        n_buf[rows, :] = n
        scale_buf[rows, :] = jnp.broadcast_to(scale, (64, 128))
        low_buf[rows, :] = (n * gain_1 + shift_1).astype(bf16)
        return carry

    for i in range(2):
        merge[i].wait_recv()
        lax.fori_loop(4 * i, 4 * i + 4, first_norm, 0)
    saves.go(n_buf, n_out)
    saves.go(scale_buf, scale_out)
    saves.go(low_buf, low_out)
    saves.wait(load_e)

    def widen(i, carry):
        at = pl.ds(pl.multiple_of(i * 256, 256), 256)
        upward = dot(low_buf[...], we[:, :, :, :, at].reshape(D, 256), NN)
        upward += bias(6 + lax.div(i, 2), me.core * 512 + lax.rem(i, 2) * 256, 256)
        gate = 0.5 + 0.5 * lax.erf(upward * math.sqrt(0.5))
        active_buf[:, at] = (upward * gate).astype(bf16)
        bell = jnp.exp(-0.5 * upward * upward) * (1.0 / math.sqrt(2.0 * math.pi))
        slope_buf[:, at] = (gate + upward * bell).astype(bf16)
        return carry

    lax.fori_loop(0, 8, widen, 0)
    saves.go(active_buf, active_out)
    saves.go(slope_buf, slope_out)
    next(go_s)
    load_s = saves.go(whole_s, ws)
    saves.wait(load_s)
    feeds = []
    for i in range(2):
        rows = pl.ds(i * 256, 256)
        found = dot(active_buf[rows, :], ws[...].reshape(2048, D), NN)
        part[rows, :] = found
        give_f[rows, :] = found.astype(bf16)
        feeds.append(wires.go(give_f.at[rows], take_f.at[rows], sibling))
    saves.wait(own_cot)
    cot_beside.wait_recv()
    bias_s, gain_2, shift_2 = bias(10, 0, D), bias(11, 0, D), bias(12, 0, D)
    small_grads[...] = jnp.zeros((16, 1024), f32)

    def second_norm(i, carry):
        rows = pl.ds(pl.multiple_of(i * 64, 64), 64)
        at = pl.ds(pl.multiple_of(lax.rem(i, 4) * 64, 64), 64)
        hidden = n_buf[rows, :] * gain_1 + shift_1
        total = hidden + part[rows, :] + take_f[rows, :].astype(f32) + bias_s
        n, scale = row_norm(total)
        upstream = ups[lax.div(i, 4), at, :].astype(f32)
        grad = row_norm_backward(upstream, gain_2, n, scale)
        second_buf[rows, :] = grad
        feed = grad.astype(bf16)
        feed_buf[rows, :] = feed

        @pl.when(lax.div(i, 4) == me.core)
        def _():
            encoded[at, :] = (n * gain_2 + shift_2).astype(bf16)
            small_grads[10:11, :] += jnp.sum(feed.astype(f32), axis=0, keepdims=True)
            small_grads[11:12, :] += jnp.sum(upstream * n, axis=0, keepdims=True)
            small_grads[12:13, :] += jnp.sum(upstream, axis=0, keepdims=True)

        return carry

    for i in range(2):
        feeds[i].wait_recv()
        lax.fori_loop(4 * i, 4 * i + 4, second_norm, 0)
    saves.go(second_buf, second_out)
    saves.go(feed_buf, feed_out)
    saves.drain()
    wires.drain()
    assert all(next(steps, "end") == "end" for steps in (go_t, go_e, go_s, go_m))

    @pl.when(mine_here)
    def _():
        z_s.wait_send()
        z_m.wait_send()


def forward_all(triple, expand, shrink, merger, small, tokens, cotangent, cosines, sines):
    shape = jax.ShapeDtypeStruct
    shapes = [
        shape((4, 2, 4, 32, 768), bf16),
        shape((4, 2, 4, 32, 2048), bf16),
        shape((4, 1, 4, 128, 1024), bf16),
        shape((4, 1, 4, 32, 1024), bf16),
        shape((4, 256, 1024), bf16),
        shape((16, 1024), f32),
        shape((256, 1024), bf16),
        shape((16, 1024), f32),
        shape((4, 1024, 1024), bf16),
        shape((2, 1024, 128), bf16),
        shape((2, 1024, 128), bf16),
        shape((2, 1024, 128), bf16),
        shape((2, 1024, 256), bf16),
        shape((2, 1024, 128), f32),
        shape((2, 2, 512, 128), bf16),
        shape((512, 1024), f32),
        shape((512, 128), f32),
        shape((512, 1024), bf16),
        shape((512, 2048), bf16),
        shape((512, 2048), bf16),
        shape((512, 1024), f32),
        shape((512, 1024), bf16),
    ]
    scratch = [
        pltpu.VMEM((3, 16, 1024), f32),
        pltpu.VMEM((3, 16, 1024), f32),
        pltpu.VMEM((16, 1024), f32),
        pltpu.VMEM((16, 1024), f32),
        pltpu.VMEM((16, 1024), f32),
        pltpu.VMEM((4, 2, 4, 32, 768), bf16),
        pltpu.VMEM((4, 2, 4, 32, 2048), bf16),
        pltpu.VMEM((4, 1, 4, 128, 1024), bf16),
        pltpu.VMEM((4, 1, 4, 32, 1024), bf16),
        pltpu.VMEM((4, 256, 1024), bf16),
        pltpu.VMEM((2, 256, 1024), bf16),
        pltpu.VMEM((4, 1024, 1024), bf16),
        pltpu.VMEM((2, 1024, 128), bf16),
        pltpu.VMEM((2, 1024, 128), bf16),
        pltpu.VMEM((2, 1024, 128), bf16),
        pltpu.VMEM((2, 1024, 256), bf16),
        pltpu.VMEM((2, 1024, 128), f32),
        pltpu.VMEM((2, 2, 512, 128), bf16),
        pltpu.VMEM((512, 1024), f32),
        pltpu.VMEM((512, 1024), bf16),
        pltpu.VMEM((512, 1024), bf16),
        pltpu.VMEM((512, 1024), bf16),
        pltpu.VMEM((512, 1024), bf16),
        pltpu.VMEM((512, 1024), f32),
        pltpu.VMEM((512, 128), f32),
        pltpu.VMEM((512, 1024), bf16),
        pltpu.VMEM((512, 2048), bf16),
        pltpu.VMEM((512, 2048), bf16),
        pltpu.VMEM((512, 1024), f32),
        pltpu.VMEM((512, 1024), bf16),
        pltpu.SemaphoreType.DMA((96,)),
        pltpu.SemaphoreType.DMA((96,)),
        pltpu.SemaphoreType.DMA((42,)),
    ]
    return pl.pallas_call(
        forward_kernel,
        out_shape=shapes,
        in_specs=[ANY, ANY, ANY, ANY, VMEM, ANY, ANY, VMEM, VMEM],
        out_specs=[ANY] * 5 + [VMEM] * 3 + [ANY] * 14,
        scratch_shapes=scratch,
        compiler_params=pltpu.CompilerParams(
            collective_id=0, has_side_effects=True, vmem_limit_bytes=58 << 20
        ),
        name="forward",
    )(triple, expand, shrink, merger, small, tokens, cotangent, cosines, sines)


NN = ((1,), (0,))
NT = ((1,), (1,))
TN = ((0,), (0,))


def reduce_steps(wires, me, grad, buffers, out):
    first_l, first_r, mid_l, mid_r, last_l, last_r = buffers
    levels, half, h = grad.shape[1], grad.shape[4] // 2, grad.shape[3] // 2
    left, right = pl.ds(0, half), pl.ds(half, half)
    upper, lower = pl.ds(0, h), pl.ds(h, h)
    on_x = (me.x, lambda i: me.at(x=i))
    on_y = (me.y, lambda i: me.at(y=i))

    def in_mid_l(n, r, value):
        mid_l[lax.div(n, levels), lax.rem(n, levels), r, :] = value

    def in_mid_r(n, r, value):
        mid_r[lax.div(n, 4), lax.rem(n, 4), r, :] = value

    def in_out_l(n, r, value):
        out[n, r, left] = value

    def in_out_r(n, r, value):
        out[n, r, right] = value

    hops = (
        (
            (
                *on_x, 4 * levels, lambda n: (lax.div(n, levels), lax.rem(n, levels)), first_l,
                lambda d, r: grad.at[:, :, d, r, left],
                lambda d, n, r: grad[lax.div(n, levels), lax.rem(n, levels), d, r, left],
                in_mid_l,
            ),
            (
                *on_y, 4 * levels, lambda n: (lax.div(n, 4), lax.rem(n, 4)), first_r,
                lambda d, r: grad.at[d, :, :, r, right],
                lambda d, n, r: grad[d, lax.div(n, 4), lax.rem(n, 4), r, right],
                in_mid_r,
            ),
        ),
        (
            (
                *on_y, levels, lambda n: (n,), last_l,
                lambda d, r: mid_l.at[d, :, r, :],
                lambda d, n, r: mid_l[d, n, r, :],
                in_out_l,
            ),
            (
                *on_x, levels, lambda n: (n,), last_r,
                lambda d, r: mid_r.at[:, d, r, :],
                lambda d, n, r: mid_r[n, d, r, :],
                in_out_r,
            ),
        ),
    )
    for hop in hops:
        sent = []
        for here, device, count, index, (relay, near, far), piece, value, store in hop:
            up, down, corner = lax.rem(here + 1, 4), lax.rem(here + 3, 4), lax.rem(here + 2, 4)
            sent.append(
                (
                    wires.go(piece(corner, upper), relay.at[0], device(up)),
                    wires.go(piece(corner, lower), relay.at[1], device(down)),
                    wires.go(piece(up, lower), near.at[0], device(up)),
                    wires.go(piece(down, upper), near.at[1], device(down)),
                )
            )
        yield
        summed = []
        for (here, device, count, index, (relay, near, far), piece, value, store), copies in zip(hop, sent):
            up, down = lax.rem(here + 1, 4), lax.rem(here + 3, 4)
            arrive(copies[:2])

            def pass_on(n, carry, relay=relay, value=value, index=index, up=up, down=down):
                at = (0, *index(n))
                relay[at] = (relay[at].astype(f32) + value(up, n, upper).astype(f32)).astype(bf16)
                at = (1, *index(n))
                relay[at] = (relay[at].astype(f32) + value(down, n, lower).astype(f32)).astype(bf16)
                return carry

            lax.fori_loop(0, count, pass_on, 0)
            summed.append(wires.go(relay.at[0], far.at[0], device(up)))
            summed.append(wires.go(relay.at[1], far.at[1], device(down)))
        yield
        arrive(summed)
        for (here, device, count, index, (relay, near, far), piece, value, store), copies in zip(hop, sent):
            arrive(copies[2:])

            def finish(n, carry, near=near, far=far, value=value, index=index, store=store, here=here):
                for r, i in ((upper, 0), (lower, 1)):
                    total = value(here, n, r).astype(f32)
                    total += near[(1 - i, *index(n))].astype(f32) + far[(i, *index(n))].astype(f32)
                    store(n, r, total.astype(bf16))
                return carry

            lax.fori_loop(0, count, finish, 0)
    yield


def reduce_scratch(levels, rows, columns):
    half, h = columns // 2, rows // 2

    def trio(*lead):
        return [pltpu.VMEM((2, *lead, h, half), bf16)] * 3

    return [
        *trio(4, levels),
        *trio(levels, 4),
        pltpu.VMEM((4, levels, rows, half), bf16),
        pltpu.VMEM((levels, 4, rows, half), bf16),
        *trio(levels),
        *trio(levels),
        pltpu.VMEM((levels, rows, columns), bf16),
    ]


def reduce_job(wires, me, grad, scratch):
    buffers = (scratch[0:3], scratch[3:6], scratch[6], scratch[7], scratch[8:11], scratch[11:14])
    return reduce_steps(wires, me, grad, buffers, scratch[14])


def backward_kernel(
    whole_t, whole_e, whole_s, whole_m, sequence, small_full, small_part,
    e_in, o_in, q_in, k_in, v_in, r_in, ctx_in, n_in, scale_in, low_in,
    active_in, slope_in, second_in, feed_in, cosines, sines,
    tokens_out, out_s, out_e, out_m, out_t, small_out, *rest,
):
    me = Place()
    scratch_s, scratch_e, scratch_m, scratch_t = (rest[15 * i : 15 * i + 15] for i in range(4))
    (
        z_s, z_e, z_m, z_t, sum_s, sum_e, sum_m, sum_t,
        small_x, small_y, small_z, small_c, sums,
        wt, we, ws, wm, e_buf, o_buf, q_buf, k_buf, v_buf, r_buf, ctx, n_buf, scale_buf,
        low_buf, active_buf, slope_buf, second_buf, feed_buf, part, take_a,
        give_c, dctx, dq_buf, pre_grad, grad_t, take_t, take_x, send, recv, local_sems,
    ) = rest[60:]
    give_a = feed_buf
    acc_k, acc_v = second_buf.at[pl.ds(0, 128)], second_buf.at[pl.ds(128, 128)]
    give_t = [active_buf.at[pl.ds(256 * z, 256), pl.ds(0, D)] for z in range(2)]
    give_x = active_buf.at[pl.ds(0, 256), pl.ds(D, D)]
    wires, saves = Wires(send, recv), Saves(local_sems)
    sibling = me.at(core=1 - me.core)
    beside, diagonal, beyond = me.z_others()
    load_feed = saves.go(feed_in, feed_buf)
    load_s = saves.go(whole_s, ws)
    load_slope = saves.go(slope_in, slope_buf)
    load_active = saves.go(active_in, active_buf)
    load_e = saves.go(whole_e, we)
    load_low = saves.go(low_in, low_buf)
    load_norm = [saves.go(n_in, n_buf), saves.go(scale_in, scale_buf), saves.go(second_in, second_buf)]
    load_m = [saves.go(whole_m, wm), saves.go(ctx_in, ctx)]
    load_heads = [
        saves.go(e_in.at[0], e_buf.at[0]), saves.go(e_in.at[1], e_buf.at[1]), saves.go(o_in, o_buf),
        saves.go(q_in, q_buf), saves.go(k_in, k_buf), saves.go(v_in, v_buf), saves.go(r_in, r_buf),
    ]
    load_t = saves.go(whole_t, wt)
    peers = [sibling, beside, diagonal, beyond, me.at(z_lo=1 - me.z_lo, core=1 - me.core)]
    peers += [me.at(x=me.along_x(k)) for k in (1, 2, 3)]
    peers += [me.at(y=me.along_y(k)) for k in (1, 2, 3)]
    meet(peers)
    go_s = reduce_job(wires, me, ws, scratch_s)
    go_e = reduce_job(wires, me, we, scratch_e)
    go_m = reduce_job(wires, me, wm, scratch_m)
    go_t = reduce_job(wires, me, grad_t, scratch_t)
    plane_s, plane_e, plane_m, plane_t = (s[14] for s in (scratch_s, scratch_e, scratch_m, scratch_t))
    sums[0] = small_part[...]

    for load in (load_feed, load_s, load_slope, load_active):
        saves.wait(load)

    def narrow(i, carry):
        y, pair = lax.div(i, 2), pl.ds(2 * lax.rem(i, 2), 2)
        at = pl.ds(pl.multiple_of(i * 256, 256), 256)
        back = dot(feed_buf[...], ws[y, 0, pair].reshape(256, D), NT)
        up = (back * slope_buf[:, at].astype(f32)).astype(bf16)
        slope_buf[:, at] = up
        where = pl.ds(pl.multiple_of(me.core * 512 + lax.rem(i, 2) * 256, 256), 256)
        sums[0, pl.ds(6 + y, 1), where] = jnp.sum(up.astype(f32), axis=0, keepdims=True)
        found = dot(active_buf[:, at], feed_buf[...], TN)
        ws[y, 0, pair] = found.astype(bf16).reshape(2, 128, D)
        return carry

    lax.fori_loop(0, 8, narrow, 0)
    next(go_s)
    saves.wait(load_e)

    def hidden_part(y, carry):
        at = pl.ds(pl.multiple_of(y * 256, 256), 256)
        found = dot(slope_buf[...], we[y].reshape(256, 2048), NT)
        part[:, at] = found
        give_a[:, at] = found.astype(bf16)
        return carry

    shared = []
    for i in range(2):
        lax.fori_loop(2 * i, 2 * i + 2, hidden_part, 0)
        at = pl.ds(512 * i, 512)
        shared.append(wires.go(give_a.at[:, at], take_a.at[:, at], sibling))
    saves.wait(load_low)

    def expand_part(i, carry):
        y, at = lax.div(i, 4), pl.ds(pl.multiple_of(lax.rem(i, 4) * 512, 512), 512)
        found = dot(low_buf[:, pl.ds(pl.multiple_of(y * 256, 256), 256)], slope_buf[:, at], TN)
        we[y, :, :, :, at] = found.astype(bf16).reshape(2, 4, 32, 512)
        return carry

    lax.fori_loop(0, 16, expand_part, 0)
    next(go_e)
    for load in load_norm:
        saves.wait(load)
    arrive(shared)
    gain_1 = small_full[4:5, :]

    def first_norm(i, carry):
        rows = pl.ds(pl.multiple_of(i * 64, 64), 64)
        upstream = part[rows, :] + take_a[rows, :].astype(f32) + second_buf[rows, :]
        n = n_buf[rows, :]
        grad = row_norm_backward(upstream, gain_1, n, scale_buf[rows, 0:1])
        n_buf[rows, :] = grad
        low = grad.astype(bf16)
        low_buf[rows, :] = low

        @pl.when(lax.div(i, 4) == me.core)
        def _():
            sums[0, 3:4, :] += jnp.sum(low.astype(f32), axis=0, keepdims=True)
            sums[0, 4:5, :] += jnp.sum(upstream * n, axis=0, keepdims=True)
            sums[0, 5:6, :] += jnp.sum(upstream, axis=0, keepdims=True)

        return carry

    lax.fori_loop(0, 8, first_norm, 0)
    for load in load_m:
        saves.wait(load)

    def context_part(group):
        return dot(low_buf[...], wm[pl.ds(2 * group, 2)].reshape(256, D), NT).astype(bf16)

    found = context_part(1 - me.z_lo)
    give_c[0] = found[:, :128]
    give_c[1] = found[:, 128:]
    chip = pl.ds(pl.multiple_of(me.z_lo * 512, 512), 512)
    swapped = wires.go(give_c, dctx.at[:, chip, :], beside)
    found = context_part(me.z_lo)
    dctx[0, chip, :] = found[:, :128]
    dctx[1, chip, :] = found[:, 128:]
    next(go_s)
    for z in range(2):
        for p in range(2):
            found = dot(ctx[z, p], low_buf[...], TN).astype(bf16)
            wm[2 * z + p] = found.reshape(1, 4, 32, D)
    next(go_m)
    for load in load_heads:
        saves.wait(load)
    swapped.wait_recv()

    def head_back(p, h):
        slot = h

        def block(i, carry):
            rows = pl.ds(pl.multiple_of(i * 256, 256), 256)
            lane = lax.broadcasted_iota(jnp.int32, (256, 128), 1)
            head = (lane >= 64) if h else (lane < 64)
            scaled = jnp.where(head, dctx[p, rows, :].astype(f32) * r_buf[p, rows, :], 0.0).astype(bf16)
            delta = jnp.sum(scaled.astype(f32) * o_buf[p, rows, :].astype(f32), axis=1, keepdims=True)
            high = delta.astype(bf16).astype(f32)
            extra = jnp.where(lane == 0, -high, jnp.where(lane == 1, high - delta, 0.0)).astype(bf16)
            given = jnp.concatenate([scaled, extra], axis=1)
            prob_grad = dot(given, v_buf[p], NT)
            powers = e_buf[slot, rows, :]
            score_grad = (powers.astype(f32) * prob_grad).astype(bf16)
            dq = dot(score_grad, k_buf[p], NN)
            if h == 0:
                dq_buf[rows, :] = dq
            else:
                dq = jnp.where(lane < 64, dq_buf[rows, :], dq)
                dq = (dq * 0.125).astype(bf16).astype(f32)
                turned = turn(dq, cosines[rows, :], -sines[rows, :])
                pre_grad[rows, pl.ds(p * 128, 128)] = turned.astype(bf16)
            q = jnp.where(head, q_buf[p, rows, :], jnp.zeros((), bf16))
            acc_k[...] += dot(q, score_grad, TN)
            acc_v[...] += dot(scaled, powers, TN)
            return carry

        lax.fori_loop(0, 4, block, 0)

    def pair_end(p):
        def block(i, carry):
            rows = pl.ds(pl.multiple_of(i * 256, 256), 256)
            dk = acc_k[:, rows].T.astype(bf16).astype(f32)
            turned = turn(dk, cosines[rows, :], -sines[rows, :])
            pre_grad[rows, pl.ds(256 + p * 128, 128)] = turned.astype(bf16)
            pre_grad[rows, pl.ds(512 + p * 128, 128)] = acc_v[:, rows].T.astype(bf16)
            return carry

        lax.fori_loop(0, 4, block, 0)

    def clear():
        acc_k[...] = jnp.zeros((128, D), f32)
        acc_v[...] = jnp.zeros((128, D), f32)

    clear()
    head_back(0, 0)
    load_2 = saves.go(e_in.at[2], e_buf.at[0])
    next(go_e)
    head_back(0, 1)
    load_3 = saves.go(e_in.at[3], e_buf.at[1])
    pair_end(0)
    clear()
    next(go_s)
    next(go_m)
    saves.wait(load_2)
    head_back(1, 0)
    seq = e_buf.at[0]
    load_seq = saves.go(sequence, seq)
    next(go_e)
    saves.wait(load_3)
    head_back(1, 1)
    pair_end(1)
    next(go_s)
    next(go_m)

    def bias_part(i, total):
        rows = pl.ds(pl.multiple_of(i * 128, 128), 128)
        return total + jnp.sum(pre_grad[rows, :].astype(f32), axis=0, keepdims=True)

    total = lax.fori_loop(0, 8, bias_part, jnp.zeros((1, 768), f32))
    for t in range(3):
        for j in range(2):
            at = pl.ds(pl.multiple_of(me.z_lo * 512 + j * 256 + me.core * 128, 128), 128)
            start = t * 256 + j * 128
            sums[0, t : t + 1, at] = total[:, start : start + 128]
    got = [wires.go(sums.at[0], small_x.at[k - 1], me.at(x=me.along_x(k))) for k in (1, 2, 3)]
    saves.wait(load_t)
    saves.wait(load_seq)

    def triple_part(y, carry):
        at = pl.ds(pl.multiple_of(y * 256, 256), 256)
        found = dot(seq[:, at], pre_grad[...], TN)
        grad_t[y] = found.astype(bf16).reshape(2, 4, 32, 768)
        return carry

    lax.fori_loop(0, 4, triple_part, 0)
    next(go_t)

    def tokens_part(z, core):
        rows = pl.ds(pl.multiple_of((2 * z + core) * 256, 256), 256)
        return dot(pre_grad[rows, :], wt[...].reshape(D, 768), NT)

    beside_rows = []
    for z in range(2):
        give_t[z][...] = tokens_part(z, 1 - me.core).astype(bf16)
        beside_rows.append(wires.go(give_t[z], take_t.at[z], sibling))
    next(go_m)
    next(go_e)
    next(go_s)
    owner = me.core == me.z_hi
    late = []

    def to_owners(plane, slots):
        copies = [
            wires.make(plane.at[0], slots.at[k], peer)
            for k, peer in enumerate((beside, diagonal, beyond))
        ]

        @pl.when(owner)
        def _():
            copies[0].start()

        @pl.when(jnp.logical_not(owner))
        def _():
            copies[1].start()
            copies[2].start()

        late.append(copies)
        return copies

    def finish_owned(plane, slots, copies, out):
        beside_copy = wires.make(out, out, sibling)

        @pl.when(owner)
        def _():
            arrive(copies)
            total = plane[0].astype(f32)
            for k in range(3):
                total += slots[k].astype(f32)
            out[...] = total.astype(bf16)
            beside_copy.start()

        return beside_copy

    copies_s = to_owners(plane_s, z_s)
    for z in range(2):
        part[pl.ds(256 * z, 256), :] = tokens_part(z, me.core)
    arrive(got)
    sums[1] = sums[0] + small_x[0] + small_x[1] + small_x[2]
    got = [wires.go(sums.at[1], small_y.at[k - 1], me.at(y=me.along_y(k))) for k in (1, 2, 3)]
    next(go_t)
    arrive(beside_rows)
    other = 1 - me.z_lo
    rows = pl.ds(pl.multiple_of(other * 256, 256), 256)
    give_x[...] = (part[rows, :] + take_t[other].astype(f32)).astype(bf16)
    across_rows = wires.go(give_x, take_x, beside)
    next(go_e)
    flip = 1 - me.z_hi
    copies_e = [
        wires.go(plane_e.at[level], z_e.at[k], peer)
        for k, (level, peer) in enumerate(((me.z_hi, beside), (flip, diagonal), (flip, beyond)))
    ]
    next(go_m)
    copies_m = to_owners(plane_m, z_m)
    next(go_t)
    arrive(got)
    sums[2] = sums[1] + small_y[0] + small_y[1] + small_y[2]
    got = [wires.go(sums.at[2], small_z.at[k], peer) for k, peer in enumerate((beside, diagonal, beyond))]
    beside_s = finish_owned(plane_s, z_s, copies_s, sum_s)
    next(go_t)
    arrive(copies_e)
    total = plane_e[me.z_hi].astype(f32)
    for k in range(3):
        total += z_e[k].astype(f32)
    sum_e[me.core] = total.astype(bf16)
    beside_e = wires.go(sum_e.at[me.core], sum_e.at[me.core], sibling)
    beside_m = finish_owned(plane_m, z_m, copies_m, sum_m)
    arrive(got)
    sums[3] = sums[2] + small_z[0] + small_z[1] + small_z[2]
    got = wires.go(sums.at[3], small_c, sibling)
    next(go_t)
    copy_t = wires.go(plane_t.at[flip], z_t, beyond)
    across_rows.wait_recv()
    rows = pl.ds(pl.multiple_of(me.z_lo * 256, 256), 256)
    own = pl.ds(pl.multiple_of(me.core * 256, 256), 256)
    tokens_out[...] = (
        part[rows, :] + take_t[me.z_lo].astype(f32) + take_x[...].astype(f32) + n_buf[own, :]
    ).astype(bf16)
    got.wait_recv()
    small_out[...] = sums[3] + small_c[...]
    copy_t.wait_recv()
    sum_t[me.seq] = (plane_t[me.z_hi].astype(f32) + z_t[...].astype(f32)).astype(bf16)
    spread = [
        wires.go(sum_t.at[me.seq], sum_t.at[me.seq], peer)
        for peer in (sibling, beside, me.at(z_lo=1 - me.z_lo, core=1 - me.core))
    ]

    @pl.when(jnp.logical_not(owner))
    def _():
        beside_s.wait_recv()
        beside_m.wait_recv()
        for copies in late:
            copies[1].wait_send()
            copies[2].wait_send()

    @pl.when(owner)
    def _():
        beside_s.wait_send()
        beside_m.wait_send()
        for copies in late:
            copies[0].wait_send()

    out_s[...] = sum_s[...].astype(f32)
    out_m[...] = sum_m[...].astype(f32)
    beside_e.wait_recv()
    for c in range(2):
        for y in range(4):
            start = y * 1024 + c * 512
            out_e[:, start : start + 512] = sum_e[c, :, y * 512 : y * 512 + 512].astype(f32)
    arrive(spread)
    for s in range(4):
        for t in range(3):
            for j in range(2):
                start = t * 1024 + (s // 2) * 512 + j * 256 + (s % 2) * 128
                cut = t * 256 + j * 128
                out_t[:, start : start + 128] = sum_t[s, :, cut : cut + 128].astype(f32)
    wires.drain()
    saves.drain()
    assert all(next(steps, "end") == "end" for steps in (go_s, go_e, go_m, go_t))


def backward_all(*operands):
    shape = jax.ShapeDtypeStruct
    shapes = [
        shape((256, 1024), bf16),
        shape((128, 1024), f32),
        shape((32, 4096), f32),
        shape((32, 1024), f32),
        shape((32, 3072), f32),
        shape((16, 1024), f32),
    ]

    def low(*dims):
        return pltpu.VMEM(dims, bf16)

    def wide(*dims):
        return pltpu.VMEM(dims, f32)

    scratch = [
        *reduce_scratch(1, 128, 1024),
        *reduce_scratch(2, 32, 2048),
        *reduce_scratch(1, 32, 1024),
        *reduce_scratch(2, 32, 768),
        low(3, 128, 1024), low(3, 32, 2048), low(3, 32, 1024), low(32, 768),
        low(128, 1024), low(2, 32, 2048), low(32, 1024), low(4, 32, 768),
        wide(3, 16, 1024), wide(3, 16, 1024), wide(3, 16, 1024), wide(16, 1024), wide(4, 16, 1024),
        low(4, 2, 4, 32, 768), low(4, 2, 4, 32, 2048), low(4, 1, 4, 128, 1024), low(4, 1, 4, 32, 1024),
        low(2, 1024, 1024), low(2, 1024, 128), low(2, 1024, 128), low(2, 1024, 128),
        low(2, 1024, 256), wide(2, 1024, 128), low(2, 2, 512, 128), wide(512, 1024), wide(512, 128),
        low(512, 1024), low(512, 2048), low(512, 2048), wide(512, 1024), low(512, 1024),
        wide(512, 1024), low(512, 1024),
        low(2, 512, 128), low(2, 1024, 128), wide(1024, 128),
        low(1024, 768), low(4, 2, 4, 32, 768),
        low(2, 256, 1024), low(256, 1024),
        pltpu.SemaphoreType.DMA((136,)),
        pltpu.SemaphoreType.DMA((136,)),
        pltpu.SemaphoreType.DMA((24,)),
    ]
    return pl.pallas_call(
        backward_kernel,
        out_shape=shapes,
        in_specs=[ANY] * 5 + [VMEM] * 2 + [ANY] * 14 + [VMEM] * 2,
        out_specs=[VMEM] * 6,
        scratch_shapes=scratch,
        compiler_params=pltpu.CompilerParams(
            collective_id=1, has_side_effects=True, vmem_limit_bytes=61 << 20
        ),
        name="backward",
    )(*operands)


def spread_small(vectors, fsdp):
    rows = []
    for v in vectors:
        n = v.shape[0]
        wide = jnp.tile(v.astype(f32), 32)
        rows.append(jnp.where(lax.iota(jnp.int32, 32 * n) // n == fsdp, wide, 0.0))
    rows.append(jnp.zeros((3 * 1024,), f32))
    return jnp.concatenate(rows).reshape(16, 1024)


def local(
    tokens, triple, triple_bias, merger, merger_bias, first_gain, first_shift,
    expand, expand_bias, shrink, shrink_bias, second_gain, second_shift, cotangent,
):
    me = Place()
    triple_cut = triple.reshape(32, 3, 2, 2, 2, 128).transpose(2, 4, 0, 1, 3, 5).reshape(2, 2, 32, 768)
    expand_cut = expand.reshape(32, 4, 2, 512).transpose(2, 0, 1, 3).reshape(2, 32, 2048)
    small = spread_small(
        (triple_bias, merger_bias, first_gain, first_shift, expand_bias, shrink_bias, second_gain, second_shift),
        me.fsdp,
    )
    inverse = 10000.0 ** (-2.0 * np.arange(32) / 64)
    angles = np.arange(LENGTH)[:, None] * inverse[None, :]
    cosines = jnp.asarray(np.tile(np.cos(angles), (1, 4)), f32)
    sines = jnp.asarray(np.tile(np.concatenate([-np.sin(angles), np.sin(angles)], axis=1), (1, 2)), f32)
    (
        whole_t, whole_e, whole_s, whole_m, sequence, small, encoded, small_part, *kept,
    ) = forward_all(
        triple_cut, expand_cut, shrink, merger, small, tokens.reshape(256, D),
        cotangent.reshape(256, D), cosines, sines,
    )
    tokens_grad, shrink_grad, expand_grad, merger_grad, triple_grad, small_sum = backward_all(
        whole_t, whole_e, whole_s, whole_m, sequence.reshape(LENGTH, D), small, small_part, *kept, cosines, sines
    )
    flat = small_sum.reshape(-1)

    def shard(start, n):
        return lax.dynamic_slice(flat, (start + me.fsdp * n,), (n,))

    return (
        encoded.reshape(1, 256, D),
        tokens_grad.reshape(1, 256, D),
        triple_grad,
        shard(0, 96),
        merger_grad,
        shard(3072, 32),
        shard(4096, 32),
        shard(5120, 32),
        expand_grad,
        shard(6144, 128),
        shrink_grad,
        shard(10240, 32),
        shard(11264, 32),
        shard(12288, 32),
    )


def solution(mesh):
    rows = P("fsdp", "seq", None)
    matrix = P("fsdp", None)
    vector = P("fsdp")
    return jax.shard_map(
        local,
        mesh=mesh,
        in_specs=(
            rows, matrix, vector, matrix, vector, vector, vector, matrix, vector, matrix, vector,
            vector, vector, rows,
        ),
        out_specs=(
            rows, rows, matrix, vector, matrix, vector, vector, vector, matrix, vector, matrix,
            vector, vector, vector,
        ),
        check_vma=False,
    )
```

profile of v0, /device:TPU:1, one launch (start us, length us, event | category | flops | bytes accessed | tf_op | source)
XLA Modules:
  0.0 208.9 jit_solution(15719984732413198681)
XLA Ops:
  0.6 0.0 copy-start.5
  0.7 0.0 copy-start.6
  0.7 0.0 copy-start.7
  0.7 0.0 copy-start.8
  0.7 0.0 copy-start.12
  0.7 0.0 copy-start.9
  0.7 0.0 copy-start.10
  0.7 0.0 copy-start.11
  0.7 1.1 reshape.69
  1.8 0.1 copy.36
  1.9 0.8 reshape.70.triple
  2.7 1.1 reshape.71
  3.9 0.1 copy.35
  4.0 0.9 reshape.72.expand
  4.8 0.0 copy-done.5
  4.9 0.1 tile.33
  4.9 0.0 copy-done.6
  5.0 0.1 tile.35
  5.0 0.0 copy-done.7
  5.1 0.1 tile.37
  5.1 0.0 copy-done.8
  5.1 0.1 tile.39
  5.2 0.0 copy-done.12
  5.2 0.0 copy-done.9
  5.3 0.1 tile.83
  5.3 0.0 copy-done.10
  5.4 0.1 tile.85
  5.4 0.0 copy-done.11
  5.4 0.1 tile.87
  5.5 0.7 reshape.73.small
  6.2 95.4 %forward.1 = (bf16[4,2,4,32,768]{4,3,2,1,0:T(8,128)(2,1)}, bf16[4,2,4,32,2048]{4,3,2,1,0:T(8,128)(2,1)}, bf16[4,1,4,128,1024]{4,3,2,1,0:T(8,128)(2,1)}, bf16[4,1...) custom-call(bf16[2,2,32,768]{3,2,1,0:T(8,128)(2,1)} %reshape.70.trip, ...), custom_call_target="tpu_custom_call" | custom-call | tf_op jit(solution)/shard_map/forward/pallas_call | solution.py:504
  101.6 0.0 copy-start
  101.6 98.9 %backward.1 = (bf16[256,1024]{1,0:T(8,128)(2,1)}, f32[128,1024]{1,0:T(8,128)}, f32[32,4096]{1,0:T(8,128)}, f32[32,1024]{1,0:T(8,128)}, f32[32,3072]{1,0:T(8,128)}, /*index=5*/f32[16,1024]{1,0:T(8,128)}) custom-call(bf16[4,2,4,32,768]{4,3,2,1,0:T(8,128)(2,1)} %get-tuple-element.43.whole_t, bf16[4,2,4,32,2048]{4,3,2,1,0:T(8,128)(2,1)} %get-tuple-element.44.whole_e, ...), custom_call_target="tpu_custom_call" | custom-call | tf_op jit(solution)/shard_map/backward/pallas_call | solution.py:1031
  200.5 0.0 copy-start.3
  200.5 0.0 copy-start.4
  200.5 0.0 copy-start.2
  200.5 0.9 copy.32
  201.4 0.6 dynamic_slice.24
  202.0 0.6 fusion.13
  202.6 0.6 dynamic_slice.28
  203.2 0.0 copy-done
  203.2 0.0 copy-start.1
  203.2 0.8 copy.51
  204.0 1.9 copy.52
  205.9 0.0 copy-done.3
  205.9 0.7 copy.53
  206.6 0.0 copy-done.4
  206.6 0.7 copy.54
  207.3 0.0 copy-done.2
  207.3 0.8 copy.55
  208.1 0.0 copy-done.1
  208.1 0.8 copy.56
  (17 shorter events, 0.1 us)
Async XLA Ops:
  0.6 4.2 %copy-start.5 = (bf16[96]{0:T(256)(128)(2,1)S(1)}, bf16[96]{0:T(256)(128)(2,1)}, u32[]{:S(2)}) copy-start(bf16[96]{0:T(256)(128)(2,1)} %param.18) | copy-start | bytes 580
  0.7 4.3 %copy-start.6 = (bf16[32]{0:T(256)(128)(2,1)S(1)}, bf16[32]{0:T(256)(128)(2,1)}, u32[]{:S(2)}) copy-start(bf16[32]{0:T(256)(128)(2,1)} %param.20) | copy-start | bytes 196
  0.7 4.4 %copy-start.7 = (bf16[32]{0:T(256)(128)(2,1)S(1)}, bf16[32]{0:T(256)(128)(2,1)}, u32[]{:S(2)}) copy-start(bf16[32]{0:T(256)(128)(2,1)} %param.21) | copy-start | bytes 196
  0.7 4.5 %copy-start.8 = (bf16[32]{0:T(256)(128)(2,1)S(1)}, bf16[32]{0:T(256)(128)(2,1)}, u32[]{:S(2)}) copy-start(bf16[32]{0:T(256)(128)(2,1)} %param.22) | copy-start | bytes 196
  0.7 4.5 %copy-start.12 = (bf16[128]{0:T(256)(128)(2,1)S(1)}, bf16[128]{0:T(256)(128)(2,1)}, u32[]{:S(2)}) copy-start(bf16[128]{0:T(256)(128)(2,1)} %param.24) | copy-start | bytes 772
  0.7 4.6 %copy-start.9 = (bf16[32]{0:T(256)(128)(2,1)S(1)}, bf16[32]{0:T(256)(128)(2,1)}, u32[]{:S(2)}) copy-start(bf16[32]{0:T(256)(128)(2,1)} %param.26) | copy-start | bytes 196
  0.7 4.6 %copy-start.10 = (bf16[32]{0:T(256)(128)(2,1)S(1)}, bf16[32]{0:T(256)(128)(2,1)}, u32[]{:S(2)}) copy-start(bf16[32]{0:T(256)(128)(2,1)} %param.27) | copy-start | bytes 196
  0.7 4.7 %copy-start.11 = (bf16[32]{0:T(256)(128)(2,1)S(1)}, bf16[32]{0:T(256)(128)(2,1)}, u32[]{:S(2)}) copy-start(bf16[32]{0:T(256)(128)(2,1)} %param.28) | copy-start | bytes 196
  101.6 101.6 %copy-start = (bf16[256,1024]{1,0:T(8,128)(2,1)S(1)}, bf16[256,1024]{1,0:T(8,128)(2,1)}, u32[]{:S(2)}) copy-start(bf16[256,1024]{1,0:T(8,128)(2,1)} %get-tuple-element.42) | copy-start | bytes 1572868
  200.5 5.4 %copy-start.3 = (f32[32,3072]{1,0:T(8,128)S(1)}, f32[32,3072]{1,0:T(8,128)}, u32[]{:S(2)}) copy-start(f32[32,3072]{1,0:T(8,128)} %get-tuple-element.92) | copy-start | bytes 1179652
  200.5 6.2 %copy-start.4 = (f32[32,1024]{1,0:T(8,128)S(1)}, f32[32,1024]{1,0:T(8,128)}, u32[]{:S(2)}) copy-start(f32[32,1024]{1,0:T(8,128)} %get-tuple-element.94) | copy-start | bytes 393220
  200.5 6.8 %copy-start.2 = (f32[32,4096]{1,0:T(8,128)S(1)}, f32[32,4096]{1,0:T(8,128)}, u32[]{:S(2)}) copy-start(f32[32,4096]{1,0:T(8,128)} %get-tuple-element.98) | copy-start | bytes 1572868
  203.2 4.9 %copy-start.1 = (f32[128,1024]{1,0:T(8,128)S(1)}, f32[128,1024]{1,0:T(8,128)}, u32[]{:S(2)}) copy-start(f32[128,1024]{1,0:T(8,128)} %get-tuple-element.100) | copy-start | bytes 1572868
where the time goes:
time: 209 us
  Pallas kernels  194 us (93%)
  local copies, waits for them, and re-layouts  13.7 us (7%)
    pallas_call x1, Pallas kernels, backward_all(): pl.pallas_call(backward_kernel, out_shape=shapes, in_specs=[ANY] * 5 + [V...  98.9 us
    pallas_call x1, Pallas kernels, forward_all(): pl.pallas_call(forward_kernel, out_shape=shapes, in_specs=[ANY, ANY, ANY,...  95.4 us
    unnamed x33, local copies, waits for them, and re-layouts  6.64 us

commit v1 on v0

--- a/solution.py
+++ b/solution.py
@@ -54,11 +54,14 @@
         ]
 
 
-def meet(peers):
+def greet(peers):
     barrier = pltpu.get_barrier_semaphore()
     for peer in peers:
         pl.semaphore_signal(barrier, inc=1, device_id=peer, device_id_type=MESH)
-    pl.semaphore_wait(barrier, len(peers))
+
+
+def meet(peers):
+    pl.semaphore_wait(pltpu.get_barrier_semaphore(), len(peers))
 
 
 class Wires:
@@ -83,6 +86,11 @@
         copy.start()
         self.open.append(copy)
         return copy
+
+    def finish(self, copies):
+        for copy in copies:
+            copy.wait()
+        self.open = [copy for copy in self.open if all(copy is not done for done in copies)]
 
     def drain(self):
         for copy in self.open:
@@ -182,12 +190,30 @@
         self.open = []
 
 
+def place_small(me, vectors, small):
+    small[...] = jnp.zeros((16, 1024), f32)
+    tile = pl.ds(pl.multiple_of(lax.div(me.fsdp, 4) * 128, 128), 128)
+    shifted = pltpu.roll(vectors[...], lax.rem(me.fsdp, 4) * 32, 1)
+    for i, row in ((1, 3), (2, 4), (3, 5), (5, 10), (6, 11), (7, 12)):
+        small[row : row + 1, tile] = shifted[i : i + 1]
+    tile = pl.ds(pl.multiple_of(lax.rem(me.fsdp, 8) * 128, 128), 128)
+    for y in range(4):
+        small[6 + y : 7 + y, tile] = jnp.where(lax.div(me.fsdp, 8) == y, vectors[4:5, :], 0.0)
+    first, ahead = lax.div(me.fsdp * 96, 128), lax.rem(me.fsdp * 96, 128)
+    shifted = pltpu.roll(vectors[...], ahead, 1)[0:1]
+    behind = lax.broadcasted_iota(jnp.int32, (1, 128), 1) >= ahead
+    for at, part in ((first, jnp.where(behind, shifted, 0.0)), (first + 1, jnp.where(behind, 0.0, shifted))):
+        tile = pl.ds(pl.multiple_of(lax.rem(at, 8) * 128, 128), 128)
+        for y in range(3):
+            small[y : y + 1, tile] += jnp.where(lax.div(at, 8) == y, part, 0.0)
+
+
 def forward_kernel(
-    triple, expand, shrink, merger, small, tokens, cotangent, cosines, sines,
+    triple, expand, shrink, merger, vectors, tokens, cotangent, cosines, sines,
     whole_t, whole_e, whole_s, whole_m, sequence, small_full, encoded, small_grads,
     e_out, o_out, q_out, k_out, v_out, r_out, ctx_out, n_out, scale_out, low_out,
     active_out, slope_out, second_out, feed_out,
-    small_x, small_y, small_z, sum_x, sum_y, wt, we, ws, wm, seq, ups,
+    small, small_x, small_y, small_z, sum_x, sum_y, wt, we, ws, wm, seq, ups,
     e_buf, o_buf, q_buf, k_buf, v_buf, r_buf, ctx, part, give_a, take_a, give_f, take_f,
     n_buf, scale_buf, low_buf, active_buf, slope_buf, second_buf, feed_buf,
     send, recv, local_sems,
@@ -200,27 +226,40 @@
     peers = [sibling, across, partner]
     peers += [me.at(x=me.along_x(k)) for k in (1, 2, 3)]
     peers += [me.at(y=me.along_y(k)) for k in (1, 2, 3)]
+    greet(peers)
+    place_small(me, vectors, small)
     meet(peers)
 
     mine_here = me.core == me.z_hi
-    slot_t = whole_t.at[me.y, me.z_hi, me.x]
-    slot_e = whole_e.at[me.y, me.z_hi, me.x]
-    slot_s = whole_s.at[me.y, 0, me.x]
-    slot_m = whole_m.at[me.y, 0, me.x]
-    z_t = wires.go(triple.at[1 - me.z_lo, me.core], slot_t, partner)
+    slot_t = wt.at[me.y, me.z_hi, me.x]
+    slot_e = we.at[me.y, me.z_hi, me.x]
+    slot_s = ws.at[me.y, 0, me.x]
+    slot_m = wm.at[me.y, 0, me.x]
+    def triple_cuts(z_lo):
+        for t in range(3):
+            for j in range(2):
+                start = pl.multiple_of(t * 1024 + z_lo * 512 + j * 256 + me.core * 128, 128)
+                yield triple.at[:, pl.ds(start, 128)], slot_t.at[:, pl.ds((j * 3 + t) * 128, 128)]
+
+    def expand_cuts():
+        for i in range(4):
+            start = pl.multiple_of(i * 1024 + me.core * 512, 512)
+            yield expand.at[:, pl.ds(start, 512)], slot_e.at[:, pl.ds(i * 512, 512)]
+
+    z_t = [wires.go(a, b, partner) for a, b in triple_cuts(1 - me.z_lo)]
     tok_across = wires.go(tokens, seq.at[me.seq], across)
     x_small = [wires.go(small, small_x.at[k - 1], me.at(x=me.along_x(k))) for k in (1, 2, 3)]
     tok_beside = wires.go(tokens, seq.at[me.seq], sibling)
-    z_e = wires.go(expand.at[me.core], slot_e, partner)
+    z_e = [wires.go(a, b, partner) for a, b in expand_cuts()]
     cot_beside = wires.go(cotangent, ups.at[me.core], sibling)
-    own_t = saves.go(triple.at[me.z_lo, me.core], slot_t)
+    own_t = [saves.go(a, b) for a, b in triple_cuts(me.z_lo)]
     own_tok = saves.go(tokens, seq.at[me.seq])
-    own_e = saves.go(expand.at[me.core], slot_e)
+    own_e = [saves.go(a, b) for a, b in expand_cuts()]
     own_cot = saves.go(cotangent, ups.at[me.core])
     z_s = wires.make(shrink, slot_s, partner)
     z_m = wires.make(merger, slot_m, partner)
-    own_s = pltpu.make_async_copy(shrink, slot_s, local_sems.at[40])
-    own_m = pltpu.make_async_copy(merger, slot_m, local_sems.at[41])
+    own_s = pltpu.make_async_copy(shrink, slot_s, local_sems.at[46])
+    own_m = pltpu.make_async_copy(merger, slot_m, local_sems.at[47])
 
     @pl.when(mine_here)
     def _():
@@ -229,24 +268,22 @@
         own_s.start()
         own_m.start()
 
-    go_t = gather_steps(wires, me, whole_t)
-    go_e = gather_steps(wires, me, whole_e)
-    go_s = gather_steps(wires, me, whole_s)
-    go_m = gather_steps(wires, me, whole_m)
-    saves.wait(own_t)
-    z_t.wait_recv()
+    go_t = gather_steps(wires, me, wt)
+    go_e = gather_steps(wires, me, we)
+    go_s = gather_steps(wires, me, ws)
+    go_m = gather_steps(wires, me, wm)
+    for copy in own_t:
+        saves.wait(copy)
+    arrive(z_t)
     next(go_t)
+    for copy in own_e:
+        saves.wait(copy)
+    arrive(z_e)
+    next(go_e)
     arrive(x_small)
     sum_x[...] = small[...] + small_x[0] + small_x[1] + small_x[2]
     y_small = [wires.go(sum_x, small_y.at[k - 1], me.at(y=me.along_y(k))) for k in (1, 2, 3)]
     next(go_t)
-    arrive(y_small)
-    sum_y[...] = sum_x[...] + small_y[0] + small_y[1] + small_y[2]
-    z_small = wires.go(sum_y, small_z, partner)
-    next(go_t)
-    saves.wait(own_e)
-    z_e.wait_recv()
-    next(go_e)
 
     @pl.when(mine_here)
     def _():
@@ -258,58 +295,62 @@
         z_s.wait_recv()
         z_m.wait_recv()
 
+    next(go_s)
     next(go_m)
+    next(go_t)
+    next(go_e)
+    arrive(y_small)
+    sum_y[...] = sum_x[...] + small_y[0] + small_y[1] + small_y[2]
+    z_small = wires.go(sum_y, small_z, partner)
+    next(go_s)
+    next(go_m)
+    next(go_e)
+    next(go_t)
+    next(go_m)
+    next(go_s)
+    z_small.wait_recv()
+    small_full[...] = sum_y[...] + small_z[...]
     tok_across.wait_recv()
     far = seq.at[(1 - me.z_lo) * 2 + me.core]
     tok_relay = wires.go(far, far, sibling)
-    z_small.wait_recv()
-    small_full[...] = sum_y[...] + small_z[...]
     next(go_t)
-    next(go_e)
-    next(go_m)
-    next(go_s)
-    next(go_t)
-    load_t = saves.go(whole_t, wt)
-    next(go_e)
-    next(go_m)
-    next(go_s)
+    saves.go(wt, whole_t)
     saves.wait(own_tok)
     arrive([tok_beside, tok_relay])
-    saves.wait(load_t)
 
     def bias(row, start, n):
         return small_full[pl.ds(row, 1), pl.ds(pl.multiple_of(start, 128), n)]
 
     bias_t = [
-        bias(t, me.z_lo * 512 + j * 256 + me.core * 128, 128) for t in range(3) for j in range(2)
+        bias(t, me.z_lo * 512 + j * 256 + me.core * 128, 128) for j in range(2) for t in range(3)
     ]
     bias_t = jnp.concatenate(bias_t, axis=1)
 
     def project(i, carry):
-        rows = pl.ds(pl.multiple_of(i * 256, 256), 256)
-        pre = dot(seq[i], wt[...].reshape(D, 768), NN) + bias_t
+        rows = pl.ds(pl.multiple_of(i * 512, 512), 512)
+        pre = dot(seq[pl.ds(2 * i, 2)].reshape(512, D), wt[...].reshape(D, 768), NN) + bias_t
         cosine, sine = cosines[rows, :], sines[rows, :]
         for p in range(2):
-            cut = pre[:, p * 128 : p * 128 + 128]
+            cut = pre[:, p * 384 : p * 384 + 128]
             q_buf[p, rows, :] = (turn(cut, cosine, sine) * 0.125).astype(bf16)
-            cut = pre[:, 256 + p * 128 : 384 + p * 128]
+            cut = pre[:, p * 384 + 128 : p * 384 + 256]
             k_buf[p, rows, :] = turn(cut, cosine, sine).astype(bf16)
-            v_buf[p, rows, pl.ds(0, 128)] = pre[:, 512 + p * 128 : 640 + p * 128].astype(bf16)
-            v_buf[p, rows, pl.ds(128, 128)] = jnp.ones((256, 128), bf16)
+            v_buf[p, rows, pl.ds(0, 128)] = pre[:, p * 384 + 256 : p * 384 + 384].astype(bf16)
+            v_buf[p, rows, pl.ds(128, 128)] = jnp.ones((512, 128), bf16)
         return carry
 
-    lax.fori_loop(0, 4, project, 0)
+    lax.fori_loop(0, 2, project, 0)
     saves.go(seq, sequence)
     saves.go(q_buf, q_out)
     saves.go(k_buf, k_out)
     saves.go(v_buf, v_out)
-    next(go_s)
     ctx_copies = []
+    keeps = []
     for p in range(2):
 
         def attend(i, carry, p=p):
-            rows = pl.ds(pl.multiple_of(i * 256, 256), 256)
-            lane = lax.broadcasted_iota(jnp.int32, (256, 128), 1)
+            rows = pl.ds(pl.multiple_of(i * 512, 512), 512)
+            lane = lax.broadcasted_iota(jnp.int32, (512, 128), 1)
             found = []
             for h in range(2):
                 head = (lane >= 64) if h else (lane < 64)
@@ -325,25 +366,23 @@
             o_buf[p, rows, :] = (jnp.where(first, found[0][:, :128], found[1][:, :128]) * over).astype(bf16)
             return carry
 
-        lax.fori_loop(0, 4, attend, 0)
+        lax.fori_loop(0, 2, attend, 0)
         saves.go(e_buf.at[pl.ds(2 * p, 2)], e_out.at[pl.ds(2 * p, 2)])
         theirs = o_buf.at[p, pl.ds(pl.multiple_of((1 - me.z_lo) * 512, 512), 512)]
         ours = o_buf.at[p, pl.ds(pl.multiple_of(me.z_lo * 512, 512), 512)]
         ctx_copies.append(wires.go(theirs, ctx.at[me.z_lo, p], across))
-        keep = saves.go(ours, ctx.at[me.z_lo, p])
+        keeps.append(saves.go(ours, ctx.at[me.z_lo, p]))
         if p == 0:
             next(go_e)
             next(go_m)
-            keep_0 = keep
     saves.go(r_buf, r_out)
     saves.go(o_buf, o_out)
     next(go_m)
-    load_m = saves.go(whole_m, wm)
+    saves.go(wm, whole_m)
     next(go_s)
-    saves.wait(keep_0)
-    saves.wait(keep)
+    for keep in keeps:
+        saves.wait(keep)
     arrive(ctx_copies)
-    saves.wait(load_m)
     ctx_rows = jnp.concatenate([ctx[0, 0], ctx[0, 1], ctx[1, 0], ctx[1, 1]], axis=1)
     merge = []
     for i in range(2):
@@ -354,7 +393,7 @@
         merge.append(wires.go(give_a.at[rows], take_a.at[rows], sibling))
     saves.go(ctx, ctx_out)
     next(go_e)
-    load_e = saves.go(whole_e, we)
+    saves.go(we, whole_e)
     bias_m, gain_1, shift_1 = bias(3, 0, D), bias(4, 0, D), bias(5, 0, D)
 
     def first_norm(i, carry):
@@ -374,24 +413,24 @@
     saves.go(n_buf, n_out)
     saves.go(scale_buf, scale_out)
     saves.go(low_buf, low_out)
-    saves.wait(load_e)
 
     def widen(i, carry):
-        at = pl.ds(pl.multiple_of(i * 256, 256), 256)
-        upward = dot(low_buf[...], we[:, :, :, :, at].reshape(D, 256), NN)
-        upward += bias(6 + lax.div(i, 2), me.core * 512 + lax.rem(i, 2) * 256, 256)
+        at = pl.ds(pl.multiple_of(i * 1024, 1024), 1024)
+        upward = dot(low_buf[...], we[:, :, :, :, at].reshape(D, 1024), NN)
+        biases = [bias(6 + 2 * i + y, me.core * 512, 512) for y in range(2)]
+        upward += jnp.concatenate(biases, axis=1)
         gate = 0.5 + 0.5 * lax.erf(upward * math.sqrt(0.5))
         active_buf[:, at] = (upward * gate).astype(bf16)
         bell = jnp.exp(-0.5 * upward * upward) * (1.0 / math.sqrt(2.0 * math.pi))
         slope_buf[:, at] = (gate + upward * bell).astype(bf16)
         return carry
 
-    lax.fori_loop(0, 8, widen, 0)
+    lax.fori_loop(0, 1, widen, 0)
+    next(go_s)
+    saves.go(ws, whole_s)
+    lax.fori_loop(1, 2, widen, 0)
     saves.go(active_buf, active_out)
     saves.go(slope_buf, slope_out)
-    next(go_s)
-    load_s = saves.go(whole_s, ws)
-    saves.wait(load_s)
     feeds = []
     for i in range(2):
         rows = pl.ds(i * 256, 256)
@@ -440,7 +479,7 @@
         z_m.wait_send()
 
 
-def forward_all(triple, expand, shrink, merger, small, tokens, cotangent, cosines, sines):
+def forward_all(triple, expand, shrink, merger, vectors, tokens, cotangent, cosines, sines):
     shape = jax.ShapeDtypeStruct
     shapes = [
         shape((4, 2, 4, 32, 768), bf16),
@@ -467,6 +506,7 @@
         shape((512, 1024), bf16),
     ]
     scratch = [
+        pltpu.VMEM((16, 1024), f32),
         pltpu.VMEM((3, 16, 1024), f32),
         pltpu.VMEM((3, 16, 1024), f32),
         pltpu.VMEM((16, 1024), f32),
@@ -497,9 +537,9 @@
         pltpu.VMEM((512, 2048), bf16),
         pltpu.VMEM((512, 1024), f32),
         pltpu.VMEM((512, 1024), bf16),
-        pltpu.SemaphoreType.DMA((96,)),
-        pltpu.SemaphoreType.DMA((96,)),
-        pltpu.SemaphoreType.DMA((42,)),
+        pltpu.SemaphoreType.DMA((104,)),
+        pltpu.SemaphoreType.DMA((104,)),
+        pltpu.SemaphoreType.DMA((48,)),
     ]
     return pl.pallas_call(
         forward_kernel,
@@ -511,7 +551,7 @@
             collective_id=0, has_side_effects=True, vmem_limit_bytes=58 << 20
         ),
         name="forward",
-    )(triple, expand, shrink, merger, small, tokens, cotangent, cosines, sines)
+    )(triple, expand, shrink, merger, vectors, tokens, cotangent, cosines, sines)
 
 
 NN = ((1,), (0,))
@@ -635,21 +675,108 @@
     return reduce_steps(wires, me, grad, buffers, scratch[14])
 
 
+def triple_steps(wires, me, grad, first_l, first_r, mid_l, mid_r, last_l, last_r, out, shares):
+    upper, lower = pl.ds(0, 16), pl.ds(16, 16)
+    one = []
+    for k in (2, 1, 3):
+        x, y = me.along_x(k), me.along_y(k)
+        one.append(wires.go(grad.at[:, :, x, upper, :], first_l.at[k - 1], me.at(x=x)))
+        one.append(wires.go(grad.at[y, :, :, lower, :], first_r.at[k - 1], me.at(y=y)))
+    yield
+    arrive(one)
+
+    def total(n, carry):
+        y, z = lax.div(n, 2), lax.rem(n, 2)
+        left = grad[y, z, me.x, upper, :].astype(f32)
+        right = grad[me.y, z, y, lower, :].astype(f32)
+        for k in range(3):
+            left += first_l[k, y, z].astype(f32)
+            right += first_r[k, z, y].astype(f32)
+        mid_l[y, z] = left.astype(bf16)
+        mid_r[z, y] = right.astype(bf16)
+        return carry
+
+    lax.fori_loop(0, 8, total, 0)
+    two = []
+    for k in range(1, 8):
+        z = 1 - me.z_hi if k % 2 else me.z_hi
+        x, y = me.along_x(k // 2), me.along_y(k // 2)
+        two.append(wires.go(mid_l.at[y, z], last_l.at[k - 1], me.at(y=y, z_hi=z)))
+        two.append(wires.go(mid_r.at[z, x], last_r.at[k - 1], me.at(x=x, z_hi=z)))
+    yield
+    arrive(two)
+    left = mid_l[me.y, me.z_hi].astype(f32)
+    right = mid_r[me.z_hi, me.x].astype(f32)
+    for k in range(7):
+        left += last_l[k].astype(f32)
+        right += last_r[k].astype(f32)
+    out[me.seq, upper, :] = left.astype(bf16)
+    out[me.seq, lower, :] = right.astype(bf16)
+    spread = [wires.go(out.at[me.seq], out.at[me.seq], peer) for peer in shares]
+    yield
+    arrive(spread)
+    yield
+
+
+def triple_scratch():
+    return [
+        pltpu.VMEM((4, 2, 4, 32, 384), bf16),
+        pltpu.VMEM((3, 4, 2, 16, 384), bf16),
+        pltpu.VMEM((3, 2, 4, 16, 384), bf16),
+        pltpu.VMEM((4, 2, 16, 384), bf16),
+        pltpu.VMEM((2, 4, 16, 384), bf16),
+        pltpu.VMEM((7, 16, 384), bf16),
+        pltpu.VMEM((7, 16, 384), bf16),
+    ]
+
+
+def small_steps(wires, me, sums, by_x, by_y, by_z, by_core, out):
+    got = [wires.go(sums.at[0], by_x.at[k - 1], me.at(x=me.along_x(k))) for k in (1, 2, 3)]
+    yield
+    arrive(got)
+    sums[1] = sums[0] + by_x[0] + by_x[1] + by_x[2]
+    got = [wires.go(sums.at[1], by_y.at[k - 1], me.at(y=me.along_y(k))) for k in (1, 2, 3)]
+    yield
+    arrive(got)
+    sums[2] = sums[1] + by_y[0] + by_y[1] + by_y[2]
+    got = [wires.go(sums.at[2], by_z.at[k], peer) for k, peer in enumerate(me.z_others())]
+    yield
+    arrive(got)
+    sums[3] = sums[2] + by_z[0] + by_z[1] + by_z[2]
+    got = wires.go(sums.at[3], by_core, me.at(core=1 - me.core))
+    yield
+    got.wait_recv()
+    out[...] = sums[3] + by_core[...]
+    yield
+
+
+def small_scratch(rows):
+    return [
+        pltpu.VMEM((4, rows, 1024), f32),
+        pltpu.VMEM((3, rows, 1024), f32),
+        pltpu.VMEM((3, rows, 1024), f32),
+        pltpu.VMEM((3, rows, 1024), f32),
+        pltpu.VMEM((rows, 1024), f32),
+    ]
+
+
 def backward_kernel(
     whole_t, whole_e, whole_s, whole_m, sequence, small_full, small_part,
     e_in, o_in, q_in, k_in, v_in, r_in, ctx_in, n_in, scale_in, low_in,
     active_in, slope_in, second_in, feed_in, cosines, sines,
-    tokens_out, out_s, out_e, out_m, out_t, small_out, *rest,
+    tokens_out, sum_s, sum_e, sum_m, sum_t, small_out, bias_out, *rest,
 ):
     me = Place()
-    scratch_s, scratch_e, scratch_m, scratch_t = (rest[15 * i : 15 * i + 15] for i in range(4))
+    scratch_s, scratch_e, scratch_m = (rest[15 * i : 15 * i + 15] for i in range(3))
+    scratch_t = (rest[45:52], rest[52:59])
+    scratch_small, scratch_bias = rest[59:64], rest[64:69]
+    sums, biases = scratch_small[0], scratch_bias[0]
     (
-        z_s, z_e, z_m, z_t, sum_s, sum_e, sum_m, sum_t,
-        small_x, small_y, small_z, small_c, sums,
+        z_s, z_e, z_m,
         wt, we, ws, wm, e_buf, o_buf, q_buf, k_buf, v_buf, r_buf, ctx, n_buf, scale_buf,
         low_buf, active_buf, slope_buf, second_buf, feed_buf, part, take_a,
-        give_c, dctx, dq_buf, pre_grad, grad_t, take_t, take_x, send, recv, local_sems,
-    ) = rest[60:]
+        give_c, dctx, dq_buf, pre_grad, take_t, take_x, send, recv, local_sems,
+    ) = rest[69:]
     give_a = feed_buf
     acc_k, acc_v = second_buf.at[pl.ds(0, 128)], second_buf.at[pl.ds(128, 128)]
     give_t = [active_buf.at[pl.ds(256 * z, 256), pl.ds(0, D)] for z in range(2)]
@@ -657,74 +784,82 @@
     wires, saves = Wires(send, recv), Saves(local_sems)
     sibling = me.at(core=1 - me.core)
     beside, diagonal, beyond = me.z_others()
-    load_feed = saves.go(feed_in, feed_buf)
-    load_s = saves.go(whole_s, ws)
-    load_slope = saves.go(slope_in, slope_buf)
-    load_active = saves.go(active_in, active_buf)
-    load_e = saves.go(whole_e, we)
-    load_low = saves.go(low_in, low_buf)
+    load_first = [
+        saves.go(feed_in, feed_buf), saves.go(whole_s, ws), saves.go(slope_in, slope_buf),
+        saves.go(active_in, active_buf),
+    ]
+    crossing = me.at(z_lo=1 - me.z_lo, core=1 - me.core)
+    peers = [sibling, beside, diagonal, beyond, crossing]
+    for z in (me.z_hi, 1 - me.z_hi):
+        peers += [me.at(x=me.along_x(k), z_hi=z) for k in (1, 2, 3)]
+        peers += [me.at(y=me.along_y(k), z_hi=z) for k in (1, 2, 3)]
+    greet(peers)
+    go_s = reduce_job(wires, me, ws, scratch_s)
+    go_e = reduce_job(wires, me, we, scratch_e)
+    go_m = reduce_job(wires, me, wm, scratch_m)
+    plane_s, plane_e, plane_m = (s[14] for s in (scratch_s, scratch_e, scratch_m))
+    go_small = small_steps(wires, me, *scratch_small, small_out)
+    go_bias = small_steps(wires, me, *scratch_bias, bias_out)
+    biases[0] = jnp.zeros((8, 1024), f32)
+    go_t = [
+        triple_steps(wires, me, *scratch_t[p], sum_t.at[p], (sibling, beside, crossing))
+        for p in range(2)
+    ]
+    sums[0] = small_part[...]
+
+    for load in load_first:
+        saves.wait(load)
+    load_e, load_low = saves.go(whole_e, we), saves.go(low_in, low_buf)
     load_norm = [saves.go(n_in, n_buf), saves.go(scale_in, scale_buf), saves.go(second_in, second_buf)]
     load_m = [saves.go(whole_m, wm), saves.go(ctx_in, ctx)]
+
+    def narrow(y, carry):
+        at = pl.ds(pl.multiple_of(y * 512, 512), 512)
+        back = dot(feed_buf[...], ws[y].reshape(512, D), NT)
+        up = (back * slope_buf[:, at].astype(f32)).astype(bf16)
+        slope_buf[:, at] = up
+        where = pl.ds(pl.multiple_of(me.core * 512, 512), 512)
+        sums[0, pl.ds(6 + y, 1), where] = jnp.sum(up.astype(f32), axis=0, keepdims=True)
+        ws[y] = dot(active_buf[:, at], feed_buf[...], TN).astype(bf16).reshape(1, 4, 128, D)
+        return carry
+
+    lax.fori_loop(0, 4, narrow, 0)
+    load_seq = [
+        saves.go(sequence.at[pl.ds(512 * i, 512)], active_buf.at[:, pl.ds(D * i, D)]) for i in range(2)
+    ]
+    meet(peers)
+    next(go_s)
+    saves.wait(load_e)
+
+    def hidden_part(i, carry):
+        at = pl.ds(pl.multiple_of(i * 512, 512), 512)
+        found = dot(slope_buf[...], we[pl.ds(2 * i, 2)].reshape(512, 2048), NT)
+        part[:, at] = found
+        give_a[:, at] = found.astype(bf16)
+        return carry
+
+    shared = []
+    for i in range(2):
+        lax.fori_loop(i, i + 1, hidden_part, 0)
+        at = pl.ds(512 * i, 512)
+        shared.append(wires.go(give_a.at[:, at], take_a.at[:, at], sibling))
+    saves.wait(load_low)
     load_heads = [
         saves.go(e_in.at[0], e_buf.at[0]), saves.go(e_in.at[1], e_buf.at[1]), saves.go(o_in, o_buf),
         saves.go(q_in, q_buf), saves.go(k_in, k_buf), saves.go(v_in, v_buf), saves.go(r_in, r_buf),
     ]
     load_t = saves.go(whole_t, wt)
-    peers = [sibling, beside, diagonal, beyond, me.at(z_lo=1 - me.z_lo, core=1 - me.core)]
-    peers += [me.at(x=me.along_x(k)) for k in (1, 2, 3)]
-    peers += [me.at(y=me.along_y(k)) for k in (1, 2, 3)]
-    meet(peers)
-    go_s = reduce_job(wires, me, ws, scratch_s)
-    go_e = reduce_job(wires, me, we, scratch_e)
-    go_m = reduce_job(wires, me, wm, scratch_m)
-    go_t = reduce_job(wires, me, grad_t, scratch_t)
-    plane_s, plane_e, plane_m, plane_t = (s[14] for s in (scratch_s, scratch_e, scratch_m, scratch_t))
-    sums[0] = small_part[...]
-
-    for load in (load_feed, load_s, load_slope, load_active):
-        saves.wait(load)
-
-    def narrow(i, carry):
-        y, pair = lax.div(i, 2), pl.ds(2 * lax.rem(i, 2), 2)
-        at = pl.ds(pl.multiple_of(i * 256, 256), 256)
-        back = dot(feed_buf[...], ws[y, 0, pair].reshape(256, D), NT)
-        up = (back * slope_buf[:, at].astype(f32)).astype(bf16)
-        slope_buf[:, at] = up
-        where = pl.ds(pl.multiple_of(me.core * 512 + lax.rem(i, 2) * 256, 256), 256)
-        sums[0, pl.ds(6 + y, 1), where] = jnp.sum(up.astype(f32), axis=0, keepdims=True)
-        found = dot(active_buf[:, at], feed_buf[...], TN)
-        ws[y, 0, pair] = found.astype(bf16).reshape(2, 128, D)
+
+    def expand_part(y, carry):
+        low = low_buf[:, pl.ds(pl.multiple_of(y * 256, 256), 256)]
+        we[y] = dot(low, slope_buf[...], TN).astype(bf16).reshape(2, 4, 32, 2048)
         return carry
 
-    lax.fori_loop(0, 8, narrow, 0)
-    next(go_s)
-    saves.wait(load_e)
-
-    def hidden_part(y, carry):
-        at = pl.ds(pl.multiple_of(y * 256, 256), 256)
-        found = dot(slope_buf[...], we[y].reshape(256, 2048), NT)
-        part[:, at] = found
-        give_a[:, at] = found.astype(bf16)
-        return carry
-
-    shared = []
-    for i in range(2):
-        lax.fori_loop(2 * i, 2 * i + 2, hidden_part, 0)
-        at = pl.ds(512 * i, 512)
-        shared.append(wires.go(give_a.at[:, at], take_a.at[:, at], sibling))
-    saves.wait(load_low)
-
-    def expand_part(i, carry):
-        y, at = lax.div(i, 4), pl.ds(pl.multiple_of(lax.rem(i, 4) * 512, 512), 512)
-        found = dot(low_buf[:, pl.ds(pl.multiple_of(y * 256, 256), 256)], slope_buf[:, at], TN)
-        we[y, :, :, :, at] = found.astype(bf16).reshape(2, 4, 32, 512)
-        return carry
-
-    lax.fori_loop(0, 16, expand_part, 0)
-    next(go_e)
+    lax.fori_loop(0, 2, expand_part, 0)
     for load in load_norm:
         saves.wait(load)
-    arrive(shared)
+    wires.finish(shared)
+    turned_buf = give_a
     gain_1 = small_full[4:5, :]
 
     def first_norm(i, carry):
@@ -734,7 +869,7 @@
         grad = row_norm_backward(upstream, gain_1, n, scale_buf[rows, 0:1])
         n_buf[rows, :] = grad
         low = grad.astype(bf16)
-        low_buf[rows, :] = low
+        turned_buf[rows, :] = low
 
         @pl.when(lax.div(i, 4) == me.core)
         def _():
@@ -745,11 +880,12 @@
         return carry
 
     lax.fori_loop(0, 8, first_norm, 0)
+    next(go_small)
     for load in load_m:
         saves.wait(load)
 
     def context_part(group):
-        return dot(low_buf[...], wm[pl.ds(2 * group, 2)].reshape(256, D), NT).astype(bf16)
+        return dot(turned_buf[...], wm[pl.ds(2 * group, 2)].reshape(256, D), NT).astype(bf16)
 
     found = context_part(1 - me.z_lo)
     give_c[0] = found[:, :128]
@@ -759,10 +895,12 @@
     found = context_part(me.z_lo)
     dctx[0, chip, :] = found[:, :128]
     dctx[1, chip, :] = found[:, 128:]
+    lax.fori_loop(2, 4, expand_part, 0)
     next(go_s)
+    next(go_e)
     for z in range(2):
         for p in range(2):
-            found = dot(ctx[z, p], low_buf[...], TN).astype(bf16)
+            found = dot(ctx[z, p], turned_buf[...], TN).astype(bf16)
             wm[2 * z + p] = found.reshape(1, 4, 32, D)
     next(go_m)
     for load in load_heads:
@@ -773,8 +911,8 @@
         slot = h
 
         def block(i, carry):
-            rows = pl.ds(pl.multiple_of(i * 256, 256), 256)
-            lane = lax.broadcasted_iota(jnp.int32, (256, 128), 1)
+            rows = pl.ds(pl.multiple_of(i * 512, 512), 512)
+            lane = lax.broadcasted_iota(jnp.int32, (512, 128), 1)
             head = (lane >= 64) if h else (lane < 64)
             scaled = jnp.where(head, dctx[p, rows, :].astype(f32) * r_buf[p, rows, :], 0.0).astype(bf16)
             delta = jnp.sum(scaled.astype(f32) * o_buf[p, rows, :].astype(f32), axis=1, keepdims=True)
@@ -791,24 +929,38 @@
                 dq = jnp.where(lane < 64, dq_buf[rows, :], dq)
                 dq = (dq * 0.125).astype(bf16).astype(f32)
                 turned = turn(dq, cosines[rows, :], -sines[rows, :])
-                pre_grad[rows, pl.ds(p * 128, 128)] = turned.astype(bf16)
+                pre_grad[p, rows, pl.ds(0, 128)] = turned.astype(bf16)
             q = jnp.where(head, q_buf[p, rows, :], jnp.zeros((), bf16))
             acc_k[...] += dot(q, score_grad, TN)
             acc_v[...] += dot(scaled, powers, TN)
             return carry
 
-        lax.fori_loop(0, 4, block, 0)
+        lax.fori_loop(0, 2, block, 0)
 
     def pair_end(p):
         def block(i, carry):
             rows = pl.ds(pl.multiple_of(i * 256, 256), 256)
             dk = acc_k[:, rows].T.astype(bf16).astype(f32)
             turned = turn(dk, cosines[rows, :], -sines[rows, :])
-            pre_grad[rows, pl.ds(256 + p * 128, 128)] = turned.astype(bf16)
-            pre_grad[rows, pl.ds(512 + p * 128, 128)] = acc_v[:, rows].T.astype(bf16)
+            pre_grad[p, rows, pl.ds(128, 128)] = turned.astype(bf16)
+            pre_grad[p, rows, pl.ds(256, 128)] = acc_v[:, rows].T.astype(bf16)
             return carry
 
         lax.fori_loop(0, 4, block, 0)
+        found = dot(active_buf[:, 0:D], pre_grad[p, 0:512, :], TN)
+        found += dot(active_buf[:, D:], pre_grad[p, 512:, :], TN)
+        scratch_t[p][0][...] = found.astype(bf16).reshape(4, 2, 4, 32, 384)
+        next(go_t[p])
+
+    def bias_part(p):
+        def block(i, total):
+            rows = pl.ds(pl.multiple_of(i * 256, 256), 256)
+            return total + jnp.sum(pre_grad[p, rows, :].astype(f32), axis=0, keepdims=True)
+
+        total = lax.fori_loop(0, 4, block, jnp.zeros((1, 384), f32))
+        at = pl.ds(pl.multiple_of(me.z_lo * 512 + p * 256 + me.core * 128, 128), 128)
+        for t in range(3):
+            biases[0, t : t + 1, at] = total[:, t * 128 : t * 128 + 128]
 
     def clear():
         acc_k[...] = jnp.zeros((128, D), f32)
@@ -818,57 +970,50 @@
     head_back(0, 0)
     load_2 = saves.go(e_in.at[2], e_buf.at[0])
     next(go_e)
+    next(go_small)
     head_back(0, 1)
     load_3 = saves.go(e_in.at[3], e_buf.at[1])
+    next(go_s)
+    for load in load_seq:
+        saves.wait(load)
     pair_end(0)
     clear()
-    next(go_s)
     next(go_m)
+    next(go_small)
     saves.wait(load_2)
     head_back(1, 0)
-    seq = e_buf.at[0]
-    load_seq = saves.go(sequence, seq)
+    next(go_t[0])
+    next(go_m)
     next(go_e)
+    next(go_s)
+    next(go_small)
     saves.wait(load_3)
     head_back(1, 1)
     pair_end(1)
+    saves.wait(load_t)
+
+    def tokens_part(z, core):
+        rows = pl.ds(pl.multiple_of((2 * z + core) * 256, 256), 256)
+        found = dot(pre_grad[0, rows, :], wt[:, :, :, :, 0:384].reshape(D, 384), NT)
+        return found + dot(pre_grad[1, rows, :], wt[:, :, :, :, 384:768].reshape(D, 384), NT)
+
+    beside_rows = []
+    for i, z in enumerate((1 - me.z_lo, me.z_lo)):
+        give_t[i][...] = tokens_part(z, 1 - me.core).astype(bf16)
+        beside_rows.append(wires.go(give_t[i], take_t.at[i], sibling))
+        if i == 0:
+            far_rows = tokens_part(z, me.core)
+            beside_rows[0].wait_recv()
+            give_x[...] = (far_rows + take_t[0].astype(f32)).astype(bf16)
+            across_rows = wires.go(give_x, take_x, beside)
+    bias_part(0)
+    bias_part(1)
+    next(go_bias)
+    part[0:256, :] = tokens_part(me.z_lo, me.core)
+    next(go_t[0])
     next(go_s)
     next(go_m)
-
-    def bias_part(i, total):
-        rows = pl.ds(pl.multiple_of(i * 128, 128), 128)
-        return total + jnp.sum(pre_grad[rows, :].astype(f32), axis=0, keepdims=True)
-
-    total = lax.fori_loop(0, 8, bias_part, jnp.zeros((1, 768), f32))
-    for t in range(3):
-        for j in range(2):
-            at = pl.ds(pl.multiple_of(me.z_lo * 512 + j * 256 + me.core * 128, 128), 128)
-            start = t * 256 + j * 128
-            sums[0, t : t + 1, at] = total[:, start : start + 128]
-    got = [wires.go(sums.at[0], small_x.at[k - 1], me.at(x=me.along_x(k))) for k in (1, 2, 3)]
-    saves.wait(load_t)
-    saves.wait(load_seq)
-
-    def triple_part(y, carry):
-        at = pl.ds(pl.multiple_of(y * 256, 256), 256)
-        found = dot(seq[:, at], pre_grad[...], TN)
-        grad_t[y] = found.astype(bf16).reshape(2, 4, 32, 768)
-        return carry
-
-    lax.fori_loop(0, 4, triple_part, 0)
-    next(go_t)
-
-    def tokens_part(z, core):
-        rows = pl.ds(pl.multiple_of((2 * z + core) * 256, 256), 256)
-        return dot(pre_grad[rows, :], wt[...].reshape(D, 768), NT)
-
-    beside_rows = []
-    for z in range(2):
-        give_t[z][...] = tokens_part(z, 1 - me.core).astype(bf16)
-        beside_rows.append(wires.go(give_t[z], take_t.at[z], sibling))
-    next(go_m)
     next(go_e)
-    next(go_s)
     owner = me.core == me.z_hi
     late = []
 
@@ -905,17 +1050,8 @@
         return beside_copy
 
     copies_s = to_owners(plane_s, z_s)
-    for z in range(2):
-        part[pl.ds(256 * z, 256), :] = tokens_part(z, me.core)
-    arrive(got)
-    sums[1] = sums[0] + small_x[0] + small_x[1] + small_x[2]
-    got = [wires.go(sums.at[1], small_y.at[k - 1], me.at(y=me.along_y(k))) for k in (1, 2, 3)]
-    next(go_t)
-    arrive(beside_rows)
-    other = 1 - me.z_lo
-    rows = pl.ds(pl.multiple_of(other * 256, 256), 256)
-    give_x[...] = (part[rows, :] + take_t[other].astype(f32)).astype(bf16)
-    across_rows = wires.go(give_x, take_x, beside)
+    next(go_t[1])
+    next(go_bias)
     next(go_e)
     flip = 1 - me.z_hi
     copies_e = [
@@ -924,12 +1060,10 @@
     ]
     next(go_m)
     copies_m = to_owners(plane_m, z_m)
-    next(go_t)
-    arrive(got)
-    sums[2] = sums[1] + small_y[0] + small_y[1] + small_y[2]
-    got = [wires.go(sums.at[2], small_z.at[k], peer) for k, peer in enumerate((beside, diagonal, beyond))]
+    next(go_bias)
+    next(go_t[1])
+    next(go_small)
     beside_s = finish_owned(plane_s, z_s, copies_s, sum_s)
-    next(go_t)
     arrive(copies_e)
     total = plane_e[me.z_hi].astype(f32)
     for k in range(3):
@@ -937,25 +1071,15 @@
     sum_e[me.core] = total.astype(bf16)
     beside_e = wires.go(sum_e.at[me.core], sum_e.at[me.core], sibling)
     beside_m = finish_owned(plane_m, z_m, copies_m, sum_m)
-    arrive(got)
-    sums[3] = sums[2] + small_z[0] + small_z[1] + small_z[2]
-    got = wires.go(sums.at[3], small_c, sibling)
-    next(go_t)
-    copy_t = wires.go(plane_t.at[flip], z_t, beyond)
-    across_rows.wait_recv()
-    rows = pl.ds(pl.multiple_of(me.z_lo * 256, 256), 256)
+    next(go_bias)
+    arrive([across_rows, beside_rows[1]])
     own = pl.ds(pl.multiple_of(me.core * 256, 256), 256)
     tokens_out[...] = (
-        part[rows, :] + take_t[me.z_lo].astype(f32) + take_x[...].astype(f32) + n_buf[own, :]
+        part[0:256, :] + take_t[1].astype(f32) + take_x[...].astype(f32) + n_buf[own, :]
     ).astype(bf16)
-    got.wait_recv()
-    small_out[...] = sums[3] + small_c[...]
-    copy_t.wait_recv()
-    sum_t[me.seq] = (plane_t[me.z_hi].astype(f32) + z_t[...].astype(f32)).astype(bf16)
-    spread = [
-        wires.go(sum_t.at[me.seq], sum_t.at[me.seq], peer)
-        for peer in (sibling, beside, me.at(z_lo=1 - me.z_lo, core=1 - me.core))
-    ]
+    next(go_t[0])
+    next(go_t[1])
+    next(go_bias)
 
     @pl.when(jnp.logical_not(owner))
     def _():
@@ -972,34 +1096,22 @@
         for copies in late:
             copies[0].wait_send()
 
-    out_s[...] = sum_s[...].astype(f32)
-    out_m[...] = sum_m[...].astype(f32)
     beside_e.wait_recv()
-    for c in range(2):
-        for y in range(4):
-            start = y * 1024 + c * 512
-            out_e[:, start : start + 512] = sum_e[c, :, y * 512 : y * 512 + 512].astype(f32)
-    arrive(spread)
-    for s in range(4):
-        for t in range(3):
-            for j in range(2):
-                start = t * 1024 + (s // 2) * 512 + j * 256 + (s % 2) * 128
-                cut = t * 256 + j * 128
-                out_t[:, start : start + 128] = sum_t[s, :, cut : cut + 128].astype(f32)
     wires.drain()
     saves.drain()
-    assert all(next(steps, "end") == "end" for steps in (go_s, go_e, go_m, go_t))
+    assert all(next(steps, "end") == "end" for steps in (go_s, go_e, go_m, *go_t, go_small, go_bias))
 
 
 def backward_all(*operands):
     shape = jax.ShapeDtypeStruct
     shapes = [
         shape((256, 1024), bf16),
-        shape((128, 1024), f32),
-        shape((32, 4096), f32),
-        shape((32, 1024), f32),
-        shape((32, 3072), f32),
+        shape((128, 1024), bf16),
+        shape((2, 32, 2048), bf16),
+        shape((32, 1024), bf16),
+        shape((2, 4, 32, 384), bf16),
         shape((16, 1024), f32),
+        shape((8, 1024), f32),
     ]
 
     def low(*dims):
@@ -1012,27 +1124,28 @@
         *reduce_scratch(1, 128, 1024),
         *reduce_scratch(2, 32, 2048),
         *reduce_scratch(1, 32, 1024),
-        *reduce_scratch(2, 32, 768),
-        low(3, 128, 1024), low(3, 32, 2048), low(3, 32, 1024), low(32, 768),
-        low(128, 1024), low(2, 32, 2048), low(32, 1024), low(4, 32, 768),
-        wide(3, 16, 1024), wide(3, 16, 1024), wide(3, 16, 1024), wide(16, 1024), wide(4, 16, 1024),
+        *triple_scratch(),
+        *triple_scratch(),
+        *small_scratch(16),
+        *small_scratch(8),
+        low(3, 128, 1024), low(3, 32, 2048), low(3, 32, 1024),
         low(4, 2, 4, 32, 768), low(4, 2, 4, 32, 2048), low(4, 1, 4, 128, 1024), low(4, 1, 4, 32, 1024),
         low(2, 1024, 1024), low(2, 1024, 128), low(2, 1024, 128), low(2, 1024, 128),
         low(2, 1024, 256), wide(2, 1024, 128), low(2, 2, 512, 128), wide(512, 1024), wide(512, 128),
         low(512, 1024), low(512, 2048), low(512, 2048), wide(512, 1024), low(512, 1024),
         wide(512, 1024), low(512, 1024),
         low(2, 512, 128), low(2, 1024, 128), wide(1024, 128),
-        low(1024, 768), low(4, 2, 4, 32, 768),
+        low(2, 1024, 384),
         low(2, 256, 1024), low(256, 1024),
-        pltpu.SemaphoreType.DMA((136,)),
-        pltpu.SemaphoreType.DMA((136,)),
+        pltpu.SemaphoreType.DMA((160,)),
+        pltpu.SemaphoreType.DMA((160,)),
         pltpu.SemaphoreType.DMA((24,)),
     ]
     return pl.pallas_call(
         backward_kernel,
         out_shape=shapes,
         in_specs=[ANY] * 5 + [VMEM] * 2 + [ANY] * 14 + [VMEM] * 2,
-        out_specs=[VMEM] * 6,
+        out_specs=[VMEM] * 7,
         scratch_shapes=scratch,
         compiler_params=pltpu.CompilerParams(
             collective_id=1, has_side_effects=True, vmem_limit_bytes=61 << 20
@@ -1041,14 +1154,41 @@
     )(*operands)
 
 
-def spread_small(vectors, fsdp):
-    rows = []
-    for v in vectors:
-        n = v.shape[0]
-        wide = jnp.tile(v.astype(f32), 32)
-        rows.append(jnp.where(lax.iota(jnp.int32, 32 * n) // n == fsdp, wide, 0.0))
-    rows.append(jnp.zeros((3 * 1024,), f32))
-    return jnp.concatenate(rows).reshape(16, 1024)
+def finish_kernel(tokens, encoded, sum_s, sum_e, sum_m, sum_t, *rest):
+    tokens_out, encoded_out, out_s, out_e, out_m, out_t = rest
+    tokens_out[...] = tokens[...]
+    encoded_out[...] = encoded[...]
+    out_s[...] = sum_s[...].astype(f32)
+    out_m[...] = sum_m[...].astype(f32)
+    for c in range(2):
+        for y in range(4):
+            start = y * 1024 + c * 512
+            out_e[:, start : start + 512] = sum_e[c, :, y * 512 : y * 512 + 512].astype(f32)
+    for s in range(4):
+        for t in range(3):
+            for j in range(2):
+                start = t * 1024 + (s // 2) * 512 + j * 256 + (s % 2) * 128
+                out_t[:, start : start + 128] = sum_t[j, s, :, t * 128 : t * 128 + 128].astype(f32)
+
+
+def finish_all(*operands):
+    shape = jax.ShapeDtypeStruct
+    shapes = [
+        shape((256, 1024), bf16),
+        shape((256, 1024), bf16),
+        shape((128, 1024), f32),
+        shape((32, 4096), f32),
+        shape((32, 1024), f32),
+        shape((32, 3072), f32),
+    ]
+    return pl.pallas_call(
+        finish_kernel,
+        out_shape=shapes,
+        in_specs=[VMEM] * 6,
+        out_specs=[VMEM] * 6,
+        compiler_params=pltpu.CompilerParams(vmem_limit_bytes=60 << 20),
+        name="finish",
+    )(*operands)
 
 
 def local(
@@ -1056,12 +1196,10 @@
     expand, expand_bias, shrink, shrink_bias, second_gain, second_shift, cotangent,
 ):
     me = Place()
-    triple_cut = triple.reshape(32, 3, 2, 2, 2, 128).transpose(2, 4, 0, 1, 3, 5).reshape(2, 2, 32, 768)
-    expand_cut = expand.reshape(32, 4, 2, 512).transpose(2, 0, 1, 3).reshape(2, 32, 2048)
-    small = spread_small(
-        (triple_bias, merger_bias, first_gain, first_shift, expand_bias, shrink_bias, second_gain, second_shift),
-        me.fsdp,
+    vectors = (
+        triple_bias, merger_bias, first_gain, first_shift, expand_bias, shrink_bias, second_gain, second_shift,
     )
+    vectors = jnp.stack([jnp.pad(v, (0, 128 - v.shape[0])) for v in vectors]).astype(f32)
     inverse = 10000.0 ** (-2.0 * np.arange(32) / 64)
     angles = np.arange(LENGTH)[:, None] * inverse[None, :]
     cosines = jnp.asarray(np.tile(np.cos(angles), (1, 4)), f32)
@@ -1069,11 +1207,14 @@
     (
         whole_t, whole_e, whole_s, whole_m, sequence, small, encoded, small_part, *kept,
     ) = forward_all(
-        triple_cut, expand_cut, shrink, merger, small, tokens.reshape(256, D),
+        triple, expand, shrink, merger, vectors, tokens.reshape(256, D),
         cotangent.reshape(256, D), cosines, sines,
     )
-    tokens_grad, shrink_grad, expand_grad, merger_grad, triple_grad, small_sum = backward_all(
+    tokens_grad, sum_s, sum_e, sum_m, sum_t, small_sum, bias_sum = backward_all(
         whole_t, whole_e, whole_s, whole_m, sequence.reshape(LENGTH, D), small, small_part, *kept, cosines, sines
+    )
+    tokens_grad, encoded, shrink_grad, expand_grad, merger_grad, triple_grad = finish_all(
+        tokens_grad, encoded, sum_s, sum_e, sum_m, sum_t
     )
     flat = small_sum.reshape(-1)
 
@@ -1084,7 +1225,7 @@
         encoded.reshape(1, 256, D),
         tokens_grad.reshape(1, 256, D),
         triple_grad,
-        shard(0, 96),
+        lax.dynamic_slice(bias_sum.reshape(-1), (me.fsdp * 96,), (96,)),
         merger_grad,
         shard(3072, 32),
         shard(4096, 32),

time: 209 us -> 203 us (0.971)
  local copies, waits for them, and re-layouts: 13.7 us -> 6.02 us
    pallas_call x1, Pallas kernels: 95.4 us -> 88 us  [forward_all(): pl.pallas_call(forward_kernel, out_shape=shapes, in_specs=[ANY, ANY, ANY,...]
    pallas_call x1, Pallas kernels: 98.9 us -> 105 us  [backward_all(): pl.pallas_call(backward_kernel, out_shape=shapes, in_specs=[ANY] * 5 + [V...]
    unnamed x33 -> x4, local copies, waits for them, and re-layouts: 6.64 us -> 0.86 us
    reshape x7 -> x0, local copies, waits for them, and re-layouts: 4.75 us -> none  [the longest x3 2.13 us: local(): expand.reshape(32, 4, 2, 512).transpose(2, 0, 1, 3).reshape(2, 32, 2048)]
    pallas_call x0 -> x1, Pallas kernels: none -> 2.94 us  [finish_all(): pl.pallas_call(finish_kernel, out_shape=shapes, in_specs=[VMEM] * 6, out_...]
    another operation x14 -> x5, local copies, waits for them, and re-layouts: 0.53 us -> 3.37 us  [local(): jnp.stack([jnp.pad(v, (0, 128 - v.shape[0])) for v in vectors]).astype(f32)]
where the time goes in v1:
time: 203 us
  Pallas kernels  196 us (97%)
  local copies, waits for them, and re-layouts  6.02 us (3%)
    pallas_call x1, Pallas kernels, backward_all(): pl.pallas_call(backward_kernel, out_shape=shapes, in_specs=[ANY] * 5 + [V...  105 us
    pallas_call x1, Pallas kernels, forward_all(): pl.pallas_call(forward_kernel, out_shape=shapes, in_specs=[ANY, ANY, ANY,...  88 us

profile of v1, /device:TPU:1, one launch (start us, length us, event | category | flops | bytes accessed | tf_op | source)
XLA Modules:
  0.0 203.0 jit_solution(3300241592302926903)
XLA Ops:
  0.6 0.7 pad_bitcast_fusion
  1.3 0.7 pad_bitcast_fusion.2
  2.0 0.7 pad_bitcast_fusion.4
  2.7 0.7 pad_bitcast_fusion.6
  3.3 0.7 stack.35
  4.0 0.6 convert_element_type.12.vectors
  4.6 88.0 %forward.1 = (bf16[4,2,4,32,768]{4,3,2,1,0:T(8,128)(2,1)}, bf16[4,2,4,32,2048]{4,3,2,1,0:T(8,128)(2,1)}, bf16[4,1,4,128,1024]{4,3,2,1,0:T(8,128)(2,1)}, bf16[4,1...) custom-call(bf16[32,3072]{1,0:T(8,128)(2,1)} %triple.1, ...), custom_call_target="tpu_custom_call" | custom-call | tf_op jit(solution)/shard_map/forward/pallas_call | solution.py:544
  92.6 104.8 %backward.1 = (bf16[256,1024]{1,0:T(8,128)(2,1)}, bf16[128,1024]{1,0:T(8,128)(2,1)}, bf16[2,32,2048]{2,1,0:T(8,128)(2,1)}, bf16[32,1024]{1,0:T(8,128)(2,1)}, bf1...) custom-call(bf16[4,2,4,32,768]{4,3,2,1,0:T(8,128)(2,1)} %get-tuple-element.49.whole_t, ...), custom_call_target="tpu_custom_call" | custom-call | tf_op jit(solution)/shard_map/backward/pallas_call | solution.py:1144
  197.4 0.0 copy-start
  197.4 2.9 %finish.1 = (bf16[256,1024]{1,0:T(8,128)(2,1)}, bf16[256,1024]{1,0:T(8,128)(2,1)}, f32[128,1024]{1,0:T(8,128)}, f32[32,4096]{1,0:T(8,128)}, f32[32,1024]{1,0:T(8,128)}, /*index=5*/f32[32,3072]{1,0:T(8,128)}) custom-call(bf16[256,1024]{1,0:T(8,128)(2,1)} %get-tuple-element.70.tokens, bf16[256,1024]{1,0:T(8,128)(2,1)} %get-tuple-element.71.encoded, ...), custom_call_target="tpu_custom_call" | custom-call | tf_op jit(solution)/shard_map/finish/pallas_call | solution.py:1184
  200.3 0.9 copy.31
  201.2 0.6 fusion
  201.8 0.6 dynamic_slice.28
  202.4 0.0 copy-done
  202.4 0.6 dynamic_slice.24
  (1 shorter events, 0.0 us)
Async XLA Ops:
  197.4 5.0 %copy-start = (f32[8,1024]{1,0:T(8,128)S(1)}, f32[8,1024]{1,0:T(8,128)}, u32[]{:S(2)}) copy-start(f32[8,1024]{1,0:T(8,128)} %get-tuple-element.79) | copy-start | bytes 98308

commit v2 on v1

--- a/solution.py
+++ b/solution.py
@@ -379,7 +379,6 @@
     saves.go(o_buf, o_out)
     next(go_m)
     saves.go(wm, whole_m)
-    next(go_s)
     for keep in keeps:
         saves.wait(keep)
     arrive(ctx_copies)
@@ -392,6 +391,7 @@
         give_a[rows, :] = found.astype(bf16)
         merge.append(wires.go(give_a.at[rows], take_a.at[rows], sibling))
     saves.go(ctx, ctx_out)
+    next(go_s)
     next(go_e)
     saves.go(we, whole_e)
     bias_m, gain_1, shift_1 = bias(3, 0, D), bias(4, 0, D), bias(5, 0, D)
@@ -969,24 +969,19 @@
     clear()
     head_back(0, 0)
     load_2 = saves.go(e_in.at[2], e_buf.at[0])
-    next(go_e)
     next(go_small)
     head_back(0, 1)
     load_3 = saves.go(e_in.at[3], e_buf.at[1])
-    next(go_s)
+    next(go_e)
     for load in load_seq:
         saves.wait(load)
     pair_end(0)
     clear()
-    next(go_m)
     next(go_small)
     saves.wait(load_2)
     head_back(1, 0)
-    next(go_t[0])
+    next(go_s)
     next(go_m)
-    next(go_e)
-    next(go_s)
-    next(go_small)
     saves.wait(load_3)
     head_back(1, 1)
     pair_end(1)
@@ -1011,9 +1006,14 @@
     next(go_bias)
     part[0:256, :] = tokens_part(me.z_lo, me.core)
     next(go_t[0])
+    next(go_e)
     next(go_s)
     next(go_m)
-    next(go_e)
+    next(go_t[1])
+    next(go_small)
+    next(go_bias)
+    next(go_t[0])
+    next(go_s)
     owner = me.core == me.z_hi
     late = []
 
@@ -1050,7 +1050,10 @@
         return beside_copy
 
     copies_s = to_owners(plane_s, z_s)
+    next(go_e)
+    next(go_m)
     next(go_t[1])
+    next(go_small)
     next(go_bias)
     next(go_e)
     flip = 1 - me.z_hi
@@ -1060,9 +1063,6 @@
     ]
     next(go_m)
     copies_m = to_owners(plane_m, z_m)
-    next(go_bias)
-    next(go_t[1])
-    next(go_small)
     beside_s = finish_owned(plane_s, z_s, copies_s, sum_s)
     arrive(copies_e)
     total = plane_e[me.z_hi].astype(f32)
@@ -1199,7 +1199,9 @@
     vectors = (
         triple_bias, merger_bias, first_gain, first_shift, expand_bias, shrink_bias, second_gain, second_shift,
     )
-    vectors = jnp.stack([jnp.pad(v, (0, 128 - v.shape[0])) for v in vectors]).astype(f32)
+    gaps = [jnp.zeros((128 - v.shape[0],), f32) for v in vectors]
+    vectors = jnp.concatenate([x for v, gap in zip(vectors, gaps) for x in (v.astype(f32), gap) if x.shape[0]])
+    vectors = vectors.reshape(8, 128)
     inverse = 10000.0 ** (-2.0 * np.arange(32) / 64)
     angles = np.arange(LENGTH)[:, None] * inverse[None, :]
     cosines = jnp.asarray(np.tile(np.cos(angles), (1, 4)), f32)

time: 203 us -> 200 us (0.985)
  Pallas kernels: 196 us -> 191 us
  local copies, waits for them, and re-layouts: 6.02 us -> 8.67 us
    concatenate x0 -> x1, local copies, waits for them, and re-layouts: none -> 6.01 us  [local(): jnp.concatenate([x for v, gap in zip(vectors, gaps) for x in (v.astype(f3...]
    pallas_call x1, Pallas kernels: 105 us -> 99.6 us  [backward_all(): pl.pallas_call(backward_kernel, out_shape=shapes, in_specs=[ANY] * 5 + [V...]
    another operation x5 -> x1, local copies, waits for them, and re-layouts: 3.37 us -> 0.01 us  [local(): jnp.stack([jnp.pad(v, (0, 128 - v.shape[0])) for v in vectors]).astype(f32)]
where the time goes in v2:
time: 200 us
  Pallas kernels  191 us (96%)
  local copies, waits for them, and re-layouts  8.67 us (4%)
    pallas_call x1, Pallas kernels, backward_all(): pl.pallas_call(backward_kernel, out_shape=shapes, in_specs=[ANY] * 5 + [V...  99.6 us
    pallas_call x1, Pallas kernels, forward_all(): pl.pallas_call(forward_kernel, out_shape=shapes, in_specs=[ANY, ANY, ANY,...  88.1 us
    concatenate x1, local copies, waits for them, and re-layouts, local(): jnp.concatenate([x for v, gap in zip(vectors, gaps) for x in (v.astype(f3...  6.01 us

profile of v2, /device:TPU:1, one launch (start us, length us, event | category | flops | bytes accessed | tf_op | source)
XLA Modules:
  0.0 200.0 jit_solution(15235437197781289547)
XLA Ops:
  0.7 6.0 %concatenate.3 = f32[1024]{0:T(1024)} concatenate(bf16[96]{0:T(256)(128)(2,1)} %param.18, f32[32]{0:T(128)S(1)} %broadcast_in_dim.3, bf16[32]{0:T(256)(128)(2,1)} %param.20, f32[96]{0:T(128)S(1)} %broadcast.3, bf16[32]{0:T(256)(128)(2,1)} %param.21, f32[96]{0:T(128)S(1)} %broadcast.3, bf16[32]{0:T(256)(128)(2,1)} %param.22, f32[96]{0:T(128)S(1)} %broadcast.3, ...), dimensions={0} | concatenate | bytes 7360 | tf_op jit(solution)/shard_map/concatenate | solution.py:1203
  6.7 88.1 %forward.1 = (bf16[4,2,4,32,768]{4,3,2,1,0:T(8,128)(2,1)}, bf16[4,2,4,32,2048]{4,3,2,1,0:T(8,128)(2,1)}, bf16[4,1,4,128,1024]{4,3,2,1,0:T(8,128)(2,1)}, bf16[4,1...) custom-call(bf16[32,3072]{1,0:T(8,128)(2,1)} %triple.1, ...), custom_call_target="tpu_custom_call" | custom-call | tf_op jit(solution)/shard_map/forward/pallas_call | solution.py:544
  94.7 99.6 %backward.1 = (bf16[256,1024]{1,0:T(8,128)(2,1)}, bf16[128,1024]{1,0:T(8,128)(2,1)}, bf16[2,32,2048]{2,1,0:T(8,128)(2,1)}, bf16[32,1024]{1,0:T(8,128)(2,1)}, bf1...) custom-call(bf16[4,2,4,32,768]{4,3,2,1,0:T(8,128)(2,1)} %get-tuple-element.49.whole_t, ...), custom_call_target="tpu_custom_call" | custom-call | tf_op jit(solution)/shard_map/backward/pallas_call | solution.py:1144
  194.3 0.0 copy-start
  194.3 2.9 %finish.1 = (bf16[256,1024]{1,0:T(8,128)(2,1)}, bf16[256,1024]{1,0:T(8,128)(2,1)}, f32[128,1024]{1,0:T(8,128)}, f32[32,4096]{1,0:T(8,128)}, f32[32,1024]{1,0:T(8,128)}, /*index=5*/f32[32,3072]{1,0:T(8,128)}) custom-call(bf16[256,1024]{1,0:T(8,128)(2,1)} %get-tuple-element.70.tokens, bf16[256,1024]{1,0:T(8,128)(2,1)} %get-tuple-element.71.encoded, ...), custom_call_target="tpu_custom_call" | custom-call | tf_op jit(solution)/shard_map/finish/pallas_call | solution.py:1184
  197.3 0.9 copy.31
  198.2 0.6 fusion
  198.8 0.6 dynamic_slice.28
  199.4 0.0 copy-done
  199.4 0.6 dynamic_slice.24
  (3 shorter events, 0.0 us)
Async XLA Ops:
  194.3 5.0 %copy-start = (f32[8,1024]{1,0:T(8,128)S(1)}, f32[8,1024]{1,0:T(8,128)}, u32[]{:S(2)}) copy-start(f32[8,1024]{1,0:T(8,128)} %get-tuple-element.79) | copy-start | bytes 98308
